TPU v7x, 512 devices: a whole 4x4x16 slice. The times are simulated.
512 devices in a mesh: ctx: 128 (over z, y, x_hi), tp: 4 (over x_lo, core).
Axes of the slice: x: 4 (x_hi: 2, x_lo: 2; x = x_hi * 2 + x_lo), y: 4, z: 16, core: 2. Of those that a mesh axis runs over, the one named last changes fastest.
Arguments:
- q_text: bfloat16 [16384, 3584], P('ctx', 'tp'), may hold values from -8 to 8, as said below
- kv_text: bfloat16 [16384, 1024], P('ctx', 'tp'), may hold values from -8 to 8, as said below
- patch_rows: bfloat16 [8192, 4608], P('ctx', 'tp'), may hold values from -6 to 6
- image_count: int32 [128], replicated, may hold values from 0 to 128, as said below
- w_out: bfloat16 [3584, 3584], P(('tp', 'ctx')), may hold values from -0.09375 to 0.09375
Outputs:
- layer_out: bfloat16 [16384, 3584], P('ctx', 'tp')
Inputs may be any that keep to these rules, and one draw needn't show every extreme that they name: `image_count`: sums to 8192; at least one shard holds only image positions. `q_text`: rows at image positions are not read. `kv_text`: rows at image positions are not read.
All inputs are finite; a program needn't handle non-finite values.
Results may differ from a plain program's by a relative error of at most 0.015.
Values may be sent and summed in bfloat16 or wider, within the bound.
A program may use at most 128 MiB of HBM per device.

v0:
```python
import jax
import jax.numpy as jnp
from jax import lax
from jax.sharding import PartitionSpec as P

HD = 128


score_scale = 0.08838834764831845


def from_partner(value, axis, bit):
    mask = 2**bit
    pairs = [(source, source ^ mask) for source in range(lax.axis_size(axis))]
    return lax.ppermute(value, axis, pairs)


def half_step(state, queries, query_pos, keys, values, key_pos):
    top, total, accum = state
    scores = (
        jnp.einsum("qhd,kd->hqk", queries, keys, preferred_element_type=jnp.float32) * score_scale
    )
    allowed = (key_pos[None, :] <= query_pos[:, None])[None]
    scores = jnp.where(allowed, scores, jnp.float32(-1e30))
    new_top = jnp.maximum(top, jnp.max(scores, axis=-1))
    expo = jnp.where(allowed, jnp.exp(scores - new_top[..., None]), jnp.float32(0.0))
    weights = expo.astype(jnp.bfloat16)
    total = jnp.sum(expo, axis=-1)
    accum = jnp.einsum("hqk,kd->hqd", weights, values, preferred_element_type=jnp.float32)
    return (new_top, total, accum)


def body(q_text, kv_text, patch_rows, image_count, w_out):
    tok = q_text.shape[0]
    qcols = q_text.shape[1]
    heads = qcols // HD
    width = patch_rows.shape[1]
    img_rows = patch_rows.shape[0]
    shards = lax.axis_size("ctx")
    me = lax.axis_index("ctx")
    cap = (tok + shards - 1) // shards
    ends = jnp.cumsum(image_count)
    starts = ends - image_count
    row_ids = jnp.arange(img_rows, dtype=jnp.int32)
    image_index = me + shards * row_ids
    target = jnp.sum((ends[None, :] <= image_index[:, None]).astype(jnp.int32), axis=1)
    below = jnp.sum((target[None, :] < target[:, None]).astype(jnp.int32), axis=1)
    slot_of = target * cap + row_ids - below
    placing = (jnp.arange(shards * cap, dtype=jnp.int32)[:, None] == slot_of[None, :]).astype(
        jnp.bfloat16
    )
    outgoing = jnp.dot(placing, patch_rows, preferred_element_type=jnp.float32).astype(jnp.bfloat16)
    incoming = lax.all_to_all(
        outgoing.reshape(shards, cap, width), "ctx", split_axis=0, concat_axis=0, tiled=True
    )
    my_count = jnp.take(image_count, me)
    my_start = jnp.take(starts, me)
    local = jnp.arange(tok, dtype=jnp.int32)
    first = tok - my_count
    is_image = local >= first
    index = jnp.clip(my_start + local - first, 0, shards * img_rows - 1)
    source = index % shards
    lowest = (my_start - source + shards - 1) // shards
    pick = source * cap + jnp.clip(index // shards - lowest, 0, cap - 1)
    picked = jnp.take(incoming.reshape(shards * cap, width), pick, axis=0)
    text = jnp.concatenate([q_text, kv_text], axis=1)
    rows = jnp.where(is_image[:, None], picked, text)
    query_all = rows[:, :qcols].reshape(tok, heads, HD)
    key_value = rows[:, qcols:]
    half = tok // 2
    steps_half = jnp.arange(half, dtype=jnp.int32)
    moved = query_all[half:]
    for bit in range(shards.bit_length() - 1):
        moved = from_partner(moved, "ctx", bit)
    queries = jnp.concatenate([query_all[:half], moved], axis=0)
    query_pos = jnp.concatenate(
        [me * tok + steps_half, (shards - 1 - me) * tok + half + steps_half]
    )
    early_q = queries[:half]
    late_q = queries[half:]
    early_pos = query_pos[:half]
    late_pos = query_pos[half:]
    early_last = jnp.max(early_pos)
    late_last = jnp.max(late_pos)

    def fresh():
        return (
            jnp.full((heads, half), -1e30, jnp.float32),
            jnp.zeros((heads, half), jnp.float32),
            jnp.zeros((heads, half, HD), jnp.float32),
        )

    piece = lax.all_gather(key_value, "ctx", axis=0, tiled=True)
    start = jnp.int32(0)
    keys = piece[:, :HD]
    values = piece[:, HD:]
    key_pos = jnp.arange(piece.shape[0], dtype=jnp.int32)
    early = lax.cond(
        start <= early_last,
        lambda state: half_step(state, early_q, early_pos, keys, values, key_pos),
        lambda state: state,
        fresh(),
    )
    late = lax.cond(
        start <= late_last,
        lambda state: half_step(state, late_q, late_pos, keys, values, key_pos),
        lambda state: state,
        fresh(),
    )
    total = jnp.concatenate([early[1], late[1]], axis=1)
    accum = jnp.concatenate([early[2], late[2]], axis=1)
    attended = (accum / total[..., None]).astype(jnp.bfloat16)
    attended = jnp.transpose(attended, (1, 0, 2)).reshape(tok, qcols)
    returned = attended[half:]
    for bit in range(shards.bit_length() - 1):
        returned = from_partner(returned, "ctx", bit)
    attended = jnp.concatenate([attended[:half], returned], axis=0)
    partial_sums = jnp.dot(
        attended,
        lax.all_gather(w_out, "ctx", axis=0, tiled=True),
        preferred_element_type=jnp.float32,
    )
    return lax.psum_scatter(
        partial_sums.astype(jnp.bfloat16), "tp", scatter_dimension=1, tiled=True
    )


def solution(mesh):
    in_specs = (P("ctx", "tp"), P("ctx", "tp"), P("ctx", "tp"), P(), P(("tp", "ctx"), None))
    out_specs = P("ctx", "tp")
    return jax.shard_map(body, mesh=mesh, in_specs=in_specs, out_specs=out_specs, check_vma=False)
```

profile of v0, /device:TPU:1, one launch (start us, length us, event | category | flops | bytes accessed | tf_op | source)
XLA Modules:
  0.0 596.4 jit_solution(1986523101706104365)
XLA Ops:
  10.6 23.0 %all-to-all-start = ((bf16[128,2,576]{2,1,0:T(2,128)(2,1)}), bf16[128,2,576]{2,1,0:T(2,128)(2,1)S(1)}, u32[]{:S(2)}, u32[]{:S(2)}) async-start(bf16[128,2,576]{2,1,0:T(2,128)(2,1)} %reshape.347), calls=%async_computation | async-start | bytes 655360 | tf_op jit(solution)/shard_map/all_to_all | solution.py:53
  37.5 16.0 %all-to-all-done = bf16[128,2,576]{2,1,0:T(2,128)(2,1)S(1)} async-done(((bf16[128,2,576]{2,1,0:T(2,128)(2,1)}), bf16[128,2,576]{2,1,0:T(2,128)(2,1)S(1)}, u32[]{:S(2)}, u32[]{:S(2)}) %all-to-all-start) | async-done | bytes 294944 | tf_op jit(solution)/shard_map/all_to_all | solution.py:53
  57.7 4.3 collective-permute-start
  64.9 4.9 collective-permute-start.1
  72.2 7.6 %collective-permute-start.2 = (bf16[64,7,128]{2,1,0:T(8,128)(2,1)S(1)}, bf16[64,7,128]{2,1,0:T(8,128)(2,1)S(1)}, u32[]{:S(2)}, u32[]{:S(2)}) collective-permute-start(bf16[64,7,128]{2,1,0:T(8,128)(2,1)S(1)} %collective-permute-done.1), channel_id=1, source_target_pairs={{0,16},{4,20},{8,24},{12,28},{16,0},{20,4},{24,8},{28,12},{32,48},... | collective-permute-start | bytes 344072 | tf_op jit(solution)/shard_map/ppermute | solution.py:15
  79.8 3.8 collective-permute-done.2
  89.3 3.8 collective-permute-start.4
  93.2 3.8 collective-permute-done.4
  97.0 4.1 collective-permute-start.5
  102.9 5.8 collective-permute-done.5
  108.7 5.7 collective-permute-start.6
  114.4 182.1 %all-gather.4.cloned.1.call-done = bf16[16384,256]{1,0:T(8,128)(2,1)} async-done(((bf16[128,256]{1,0:T(8,128)(2,1)}), bf16[16384,256]{1,0:T(8,128)(2,1)}) %all-gather.4.cloned.1.call-update) | async-done | bytes 8388624 | tf_op jit(solution)/shard_map/all_gather | solution.py:93
  296.5 5.8 fusion.38
  302.3 43.6 %conditional.2 = (f32[7,64]{1,0:T(8,128)S(1)}, f32[7,64,128]{2,1,0:T(8,128)S(1)}) conditional(s32[]{:T(128)} %convert_element_type.28, () %tuple.21, (s32[16384]{0:T(1024)S(1)}, s32[64]{0:T(128)S(1)}, bf16[128,1152]{1,0:T(8,128)(2,1)S(1)}, bf16[16384,128]{1,0:T(8,128)(2,1)}, bf16[16384,128]{1,0:T(8,128)(2,1)}) %tuple.22), branch_computations={%region_4.5_spmd, %region_5.8_spmd} | conditional | flops 3854564864 | bytes 101083920 | solution.py:98
  303.2 13.7 %fusion = (f32[7,64]{1,0:T(8,128)S(1)}, f32[16384,64,7]{0,1,2:T(8,128)}) fusion(pred[64,16384]{1,0:T(8,128)(4,1)S(1)} %broadcast_compare_fusion, bf16[16384,128]{1,0:T(8,128)(2,1)} %get-tuple-element.29, bf16[128,1152]{1,0:T(8,128)(2,1)S(1)} %get-tuple-element.30), kind=kOutput, calls=%fused_computation.3 | convolution fusion | flops 1901067776 | bytes 34719488 | tf_op jit(solution)/shard_map/cond/branch_1_fun/qhd,kd->hqk/dot_general | solution.py:21
  316.9 14.6 %fusion.3 = f32[7,64,128]{2,1,0:T(8,128)S(1)} fusion(f32[16384,64,7]{0,1,2:T(8,128)} %get-tuple-element.88, f32[7,64]{1,0:T(8,128)S(1)} %broadcast_maximum_fusion, pred[64,16384]{1,0:T(8,128)(4,1)S(1)} %broadcast_compare_fusion, bf16[16384,128]{1,0:T(8,128)(2,1)} %get-tuple-element.31), kind=kOutput, calls=%fused_computation.6 | convolution fusion | flops 1915748352 | bytes 34834176 | tf_op jit(solution)/shard_map/cond/branch_1_fun/hqk,kd->hqd/dot_general | solution.py:29
  331.5 14.4 %fusion.2 = f32[7,64]{1,0:T(8,128)S(1)} fusion(f32[16384,64,7]{0,1,2:T(8,128)} %get-tuple-element.88, f32[7,64]{1,0:T(8,128)S(1)} %broadcast_maximum_fusion, pred[64,16384]{1,0:T(8,128)(4,1)S(1)} %broadcast_compare_fusion), kind=kLoop, calls=%fused_computation.5 | loop fusion | flops 36699712 | bytes 30412288 | tf_op jit(solution)/shard_map/cond/branch_1_fun/reduce_sum | solution.py:28
  346.0 43.8 %conditional.3 = (f32[7,64]{1,0:T(8,128)S(1)}, f32[7,64,128]{2,1,0:T(8,128)S(1)}) conditional(s32[]{:T(128)} %convert_element_type.32, () %tuple.23, (s32[16384]{0:T(1024)S(1)}, s32[64]{0:T(128)S(1)}, bf16[16384,128]{1,0:T(8,128)(2,1)}, bf16[64,7,128]{2,1,0:T(8,128)(2,1)S(1)}, bf16[16384,128]{1,0:T(8,128)(2,1)}) %tuple.24), branch_computations={%region_9.10_spmd, %region_10.13_spmd} | conditional | flops 3854564864 | bytes 101083920 | solution.py:104
  346.8 14.0 %fusion.14 = (f32[7,64]{1,0:T(8,128)S(1)}, f32[16384,64,7]{0,1,2:T(8,128)}) fusion(pred[64,16384]{1,0:T(8,128)(4,1)S(1)} %broadcast_compare_fusion.1, bf16[64,7,128]{2,1,0:T(8,128)(2,1)S(1)} %get-tuple-element.85, bf16[16384,128]{1,0:T(8,128)(2,1)} %get-tuple-element.34), kind=kOutput, calls=%fused_computation.21 | convolution fusion | flops 1901067776 | bytes 34719488 | tf_op jit(solution)/shard_map/cond/branch_1_fun/qhd,kd->hqk/dot_general | solution.py:21
  360.8 14.6 %fusion.17 = f32[7,64,128]{2,1,0:T(8,128)S(1)} fusion(f32[16384,64,7]{0,1,2:T(8,128)} %get-tuple-element.90, f32[7,64]{1,0:T(8,128)S(1)} %broadcast_maximum_fusion.1, pred[64,16384]{1,0:T(8,128)(4,1)S(1)} %broadcast_compare_fusion.1, bf16[16384,128]{1,0:T(8,128)(2,1)} %get-tuple-element.36), kind=kOutput, calls=%fused_computation.24 | convolution fusion | flops 1915748352 | bytes 34834176 | tf_op jit(solution)/shard_map/cond/branch_1_fun/hqk,kd->hqd/dot_general | solution.py:29
  375.4 14.4 %fusion.16 = f32[7,64]{1,0:T(8,128)S(1)} fusion(f32[16384,64,7]{0,1,2:T(8,128)} %get-tuple-element.90, f32[7,64]{1,0:T(8,128)S(1)} %broadcast_maximum_fusion.1, pred[64,16384]{1,0:T(8,128)(4,1)S(1)} %broadcast_compare_fusion.1), kind=kLoop, calls=%fused_computation.23 | loop fusion | flops 36699712 | bytes 30412288 | tf_op jit(solution)/shard_map/cond/branch_1_fun/reduce_sum | solution.py:28
  392.3 7.7 %collective-permute-done.7 = bf16[64,896]{1,0:T(8,128)(2,1)S(1)} collective-permute-done((bf16[64,896]{1,0:T(8,128)(2,1)S(1)}, bf16[64,896]{1,0:T(8,128)(2,1)S(1)}, u32[]{:S(2)}, u32[]{:S(2)}) %collective-permute-start.7) | collective-permute-done | bytes 114720 | tf_op jit(solution)/shard_map/ppermute | solution.py:15
  405.7 5.2 collective-permute-start.9
  416.0 3.7 collective-permute-done.10
  422.8 5.5 collective-permute-done.11
  428.3 5.7 collective-permute-start.12
  434.0 7.9 %collective-permute-done.12 = bf16[64,896]{1,0:T(8,128)(2,1)S(1)} collective-permute-done((bf16[64,896]{1,0:T(8,128)(2,1)S(1)}, bf16[64,896]{1,0:T(8,128)(2,1)S(1)}, u32[]{:S(2)}, u32[]{:S(2)}) %collective-permute-start.12) | collective-permute-done | bytes 114720 | tf_op jit(solution)/shard_map/ppermute | solution.py:15
  441.9 4.9 collective-permute-start.13
  446.8 96.4 %all-gather.6.cloned.1.call-done = bf16[128,7,3584]{2,1,0:T(8,128)(2,1)} async-done(((bf16[1,7,3584]{2,1,0:T(8,128)(2,1)}), bf16[128,7,3584]{2,1,0:T(8,128)(2,1)}) %all-gather.6.cloned.1.call-update) | async-done | bytes 6422544 | tf_op jit(solution)/shard_map/all_gather | solution.py:120
  543.2 8.8 %reshape.339 = bf16[896,3584]{1,0:T(8,128)(2,1)} reshape(bf16[128,7,3584]{2,1,0:T(8,128)(2,1)} %all-gather.6.cloned.1.call-done) | data formatting | bytes 12845056
  552.1 3.9 convolution_convert_fusion
  557.4 30.8 %reduce-scatter.4.cloned.1.call-done = bf16[896,128]{1,0:T(8,128)(2,1)} async-done(((bf16[3584,128]{1,0:T(8,128)(2,1)}), bf16[896,128]{1,0:T(8,128)(2,1)}) %reduce-scatter.4.cloned.1.call-update) | async-done | bytes 229392
  (62 shorter events, 43.2 us)
Async XLA Ops:
  6.5 1.5 copy-start
  10.6 42.8 %all-to-all-start = ((bf16[128,2,576]{2,1,0:T(2,128)(2,1)}), bf16[128,2,576]{2,1,0:T(2,128)(2,1)S(1)}, u32[]{:S(2)}, u32[]{:S(2)}) async-start(bf16[128,2,576]{2,1,0:T(2,128)(2,1)} %reshape.347), calls=%async_computation | async-start | bytes 655360 | tf_op jit(solution)/shard_map/all_to_all | solution.py:53
  33.5 263.0 %all-gather.4.cloned.1.call-start = ((), (), s32[]{:S(2)}) async-start(), calls=%async_computation.2 | async-start | bytes 8454144 | tf_op jit(solution)/shard_map/all_gather | solution.py:93
  56.7 486.5 %all-gather.6.cloned.1.call-start = ((), (), s32[]{:S(2)}) async-start(), calls=%async_computation.3 | async-start | bytes 7397376 | tf_op jit(solution)/shard_map/all_gather | solution.py:120
  57.5 530.7 %reduce-scatter.4.cloned.1.call-start = ((), (), s32[]{:S(2)}) async-start(), calls=%async_computation.4 | async-start | bytes 1146880
  57.7 7.2 %collective-permute-start = (bf16[64,7,128]{2,1,0:T(8,128)(2,1)S(1)}, bf16[64,7,128]{2,1,0:T(8,128)(2,1)S(1)}, u32[]{:S(2)}, u32[]{:S(2)}) collective-permute-start(bf16[64,7,128]{2,1,0:T(8,128)(2,1)S(1)} %slice.41), channel_id=1, source_target_pairs={{0,4},{4,0},{8,12},{12,8},{16,20},{20,16},{24,28},{28,24},{32,36},... | collective-permute-start | bytes 344072 | tf_op jit(solution)/shard_map/ppermute | solution.py:15
  64.9 7.3 %collective-permute-start.1 = (bf16[64,7,128]{2,1,0:T(8,128)(2,1)S(1)}, bf16[64,7,128]{2,1,0:T(8,128)(2,1)S(1)}, u32[]{:S(2)}, u32[]{:S(2)}) collective-permute-start(bf16[64,7,128]{2,1,0:T(8,128)(2,1)S(1)} %collective-permute-done), channel_id=1, source_target_pairs={{0,8},{4,12},{8,0},{12,4},{16,24},{20,28},{24,16},{28,20},{32,40},... | collective-permute-start | bytes 344072 | tf_op jit(solution)/shard_map/ppermute | solution.py:15
  72.2 11.4 %collective-permute-start.2 = (bf16[64,7,128]{2,1,0:T(8,128)(2,1)S(1)}, bf16[64,7,128]{2,1,0:T(8,128)(2,1)S(1)}, u32[]{:S(2)}, u32[]{:S(2)}) collective-permute-start(bf16[64,7,128]{2,1,0:T(8,128)(2,1)S(1)} %collective-permute-done.1), channel_id=1, source_target_pairs={{0,16},{4,20},{8,24},{12,28},{16,0},{20,4},{24,8},{28,12},{32,48},... | collective-permute-start | bytes 344072 | tf_op jit(solution)/shard_map/ppermute | solution.py:15
  83.5 5.8 collective-permute-start.3
  89.3 7.6 %collective-permute-start.4 = (bf16[64,7,128]{2,1,0:T(8,128)(2,1)S(1)}, bf16[64,7,128]{2,1,0:T(8,128)(2,1)S(1)}, u32[]{:S(2)}, u32[]{:S(2)}) collective-permute-start(bf16[64,7,128]{2,1,0:T(8,128)(2,1)S(1)} %collective-permute-done.3), channel_id=1, source_target_pairs={{0,64},{4,68},{8,72},{12,76},{16,80},{20,84},{24,88},{28,92},{32,9... | collective-permute-start | bytes 344072 | tf_op jit(solution)/shard_map/ppermute | solution.py:15
  97.0 11.7 %collective-permute-start.5 = (bf16[64,7,128]{2,1,0:T(8,128)(2,1)S(1)}, bf16[64,7,128]{2,1,0:T(8,128)(2,1)S(1)}, u32[]{:S(2)}, u32[]{:S(2)}) collective-permute-start(bf16[64,7,128]{2,1,0:T(8,128)(2,1)S(1)} %collective-permute-done.4), channel_id=1, source_target_pairs={{0,128},{4,132},{8,136},{12,140},{16,144},{20,148},{24,152},{28,15... | collective-permute-start | bytes 344072 | tf_op jit(solution)/shard_map/ppermute | solution.py:15
  108.7 237.3 %collective-permute-start.6 = (bf16[64,7,128]{2,1,0:T(8,128)(2,1)S(1)}, bf16[64,7,128]{2,1,0:T(8,128)(2,1)S(1)}, u32[]{:S(2)}, u32[]{:S(2)}) collective-permute-start(bf16[64,7,128]{2,1,0:T(8,128)(2,1)S(1)} %collective-permute-done.5), channel_id=1, source_target_pairs={{0,256},{4,260},{8,264},{12,268},{16,272},{20,276},{24,280},{28,28... | collective-permute-start | bytes 344072 | tf_op jit(solution)/shard_map/ppermute | solution.py:15
  389.8 200.1 %copy-start.1 = (bf16[64,1152]{1,0:T(8,128)(2,1)S(1)}, bf16[64,1152]{1,0:T(8,128)(2,1)}, u32[]{:S(2)}) copy-start(bf16[64,1152]{1,0:T(8,128)(2,1)} %param.11) | copy-start | bytes 442372
  390.1 9.9 %collective-permute-start.7 = (bf16[64,896]{1,0:T(8,128)(2,1)S(1)}, bf16[64,896]{1,0:T(8,128)(2,1)S(1)}, u32[]{:S(2)}, u32[]{:S(2)}) collective-permute-start(bf16[64,896]{1,0:T(8,128)(2,1)S(1)} %bitcast.79), channel_id=1, source_target_pairs={{0,4},{4,0},{8,12},{12,8},{16,20},{20,16},{24,28},{28,24},{32,36},... | collective-permute-start | bytes 344072 | tf_op jit(solution)/shard_map/ppermute | solution.py:15
  400.0 5.7 collective-permute-start.8
  405.7 8.0 %collective-permute-start.9 = (bf16[64,896]{1,0:T(8,128)(2,1)S(1)}, bf16[64,896]{1,0:T(8,128)(2,1)S(1)}, u32[]{:S(2)}, u32[]{:S(2)}) collective-permute-start(bf16[64,896]{1,0:T(8,128)(2,1)S(1)} %collective-permute-done.8), channel_id=1, source_target_pairs={{0,16},{4,20},{8,24},{12,28},{16,0},{20,4},{24,8},{28,12},{32,48},... | collective-permute-start | bytes 344072 | tf_op jit(solution)/shard_map/ppermute | solution.py:15
  413.7 6.0 %collective-permute-start.10 = (bf16[64,896]{1,0:T(8,128)(2,1)S(1)}, bf16[64,896]{1,0:T(8,128)(2,1)S(1)}, u32[]{:S(2)}, u32[]{:S(2)}) collective-permute-start(bf16[64,896]{1,0:T(8,128)(2,1)S(1)} %collective-permute-done.9), channel_id=1, source_target_pairs={{0,32},{4,36},{8,40},{12,44},{16,48},{20,52},{24,56},{28,60},{32,0... | collective-permute-start | bytes 344072 | tf_op jit(solution)/shard_map/ppermute | solution.py:15
  419.7 8.6 %collective-permute-start.11 = (bf16[64,896]{1,0:T(8,128)(2,1)S(1)}, bf16[64,896]{1,0:T(8,128)(2,1)S(1)}, u32[]{:S(2)}, u32[]{:S(2)}) collective-permute-start(bf16[64,896]{1,0:T(8,128)(2,1)S(1)} %collective-permute-done.10), channel_id=1, source_target_pairs={{0,64},{4,68},{8,72},{12,76},{16,80},{20,84},{24,88},{28,92},{32,9... | collective-permute-start | bytes 344072 | tf_op jit(solution)/shard_map/ppermute | solution.py:15
  428.3 13.6 %collective-permute-start.12 = (bf16[64,896]{1,0:T(8,128)(2,1)S(1)}, bf16[64,896]{1,0:T(8,128)(2,1)S(1)}, u32[]{:S(2)}, u32[]{:S(2)}) collective-permute-start(bf16[64,896]{1,0:T(8,128)(2,1)S(1)} %collective-permute-done.11), channel_id=1, source_target_pairs={{0,128},{4,132},{8,136},{12,140},{16,144},{20,148},{24,152},{28,15... | collective-permute-start | bytes 344072 | tf_op jit(solution)/shard_map/ppermute | solution.py:15
  441.9 110.2 %collective-permute-start.13 = (bf16[64,896]{1,0:T(8,128)(2,1)S(1)}, bf16[64,896]{1,0:T(8,128)(2,1)S(1)}, u32[]{:S(2)}, u32[]{:S(2)}) collective-permute-start(bf16[64,896]{1,0:T(8,128)(2,1)S(1)} %collective-permute-done.12), channel_id=1, source_target_pairs={{0,256},{4,260},{8,264},{12,268},{16,272},{20,276},{24,280},{28,28... | collective-permute-start | bytes 344072 | tf_op jit(solution)/shard_map/ppermute | solution.py:15
Sparse Core Ops, SparseCore 0:
  56.8 239.6 all-gather.3
  301.0 242.1 all-gather.5
  557.5 30.6 reduce-scatter.3
where the time goes:
time: 598 us; the launch traced here: 596 us
  waiting for transfers between devices  377 us (63%)
  starting transfers between devices  83.8 us (14%)
  matrix products  61.1 us (10%)
  other arithmetic  34.3 us (6%)
  local copies, waits for them, and re-layouts  24.2 us (4%)
  between operations  15.9 us (3%)
    all_gather x1, waiting for transfers between devices, body(): piece = lax.all_gather(key_value, 'ctx', axis=0, tiled=True)  182 us
    all_gather x1, waiting for transfers between devices, body(): lax.all_gather(w_out, 'ctx', axis=0, tiled=True)  96.4 us
    ppermute x14, starting transfers between devices, from_partner(): return lax.ppermute(value, axis, pairs)  60.7 us
    ppermute x14, waiting for transfers between devices, from_partner(): return lax.ppermute(value, axis, pairs)  50.7 us
    unnamed x4, waiting for transfers between devices  31.5 us
    dot_general x2, matrix products, half_step(): jnp.einsum('hqk,kd->hqd', weights, values, preferred_element_type=jnp.flo...  29.2 us
    reduce_sum x2, other arithmetic, half_step(): total = jnp.sum(expo, axis=-1)  28.9 us
    dot_general x2, matrix products, half_step(): jnp.einsum('qhd,kd->hqk', queries, keys, preferred_element_type=jnp.float32)  27.7 us
  transfers between devices with their start and end apart: 18, of which 16 were waited for; matrix products, arithmetic and copies ran while one was open for 18% of the time, Pallas kernels for 0%

commit v1 on v0

v1 whole, which is shorter than its diff:
```python
import functools

import jax
import jax.numpy as jnp
from jax import lax
from jax.experimental import pallas as pl
from jax.experimental.pallas import tpu as pltpu
from jax.sharding import PartitionSpec as P

HD = 128
HEADS = 7
BLK = 128
NZ, NY = 16, 4
BF = jnp.bfloat16
F32 = jnp.float32
NT = (((1,), (1,)), ((), ()))
SCORE_SCALE = 0.08838834764831845 * 1.4426950408889634
MESH = pl.DeviceIdType.MESH


def attention_kernel(
    q_ref, kv_ref, out_ref, buf, top, acc,
    z_send, z_recv, y_send, y_recv, h_send, h_recv, sib_send, sib_recv,
):
    ctx = lax.axis_index("ctx")
    tp = lax.axis_index("tp")
    z, y, xh = ctx // 8, (ctx // 2) % 4, ctx % 2
    xl, core = tp // 2, tp % 2
    y_up, y_down, y_far = (y + 1) % 4, (y + 3) % 4, (y + 2) % 4

    def device(z_, y_, core_):
        return ((z_ * 4 + y_) * 2 + xh, xl * 2 + core_)

    def copy(src, dst, send, recv, z_, y_, core_):
        return pltpu.make_async_remote_copy(
            src_ref=src, dst_ref=dst, send_sem=send, recv_sem=recv,
            device_id=device(z_, y_, core_), device_id_type=MESH,
        )

    def z_copy(way, step, group, kind):
        part = buf.at[0, group, y] if kind == 0 else buf.at[1, group]
        z_to = (z + 17 - 2 * way) % NZ
        return copy(part, part, z_send.at[way, step], z_recv.at[group], z_to, y, core)

    def y_copy(way, group, kind):
        part = buf.at[kind, group, y]
        return copy(part, part, y_send.at[way, group], y_recv.at[way, group],
                    z, (y + 1 + 2 * way) % 4, core)

    def far_copy(group):
        part = buf.at[1, group, y]
        return copy(part, part, h_send.at[0, group], h_recv.at[0, group], z, y_far, core)

    def half_copy(way, group):
        rows = pl.ds(way * 64, 64)
        part = buf.at[0, group, (y + 3 + 2 * way) % 4, rows]
        return copy(part, part, h_send.at[way, group], h_recv.at[way, group],
                    z, (y + 1 + 2 * way) % 4, core)

    def sib_copy(group):
        part = buf.at[core, group]
        return copy(part, part, sib_send.at[group], sib_recv.at[group], z, y, 1 - core)

    def group_at(way, step):
        return (z + NZ - step + 2 * step * way) % NZ

    barrier = pltpu.get_barrier_semaphore()
    for z_, y_, core_ in (
        ((z + 1) % NZ, y, core), ((z + NZ - 1) % NZ, y, core),
        (z, y_up, core), (z, y_down, core), (z, y_far, core), (z, y, 1 - core),
    ):
        pl.semaphore_signal(barrier, inc=1, device_id=device(z_, y_, core_), device_id_type=MESH)
    buf[core, z, y] = kv_ref[...]
    top[...] = jnp.full_like(top, -1e30)
    acc[...] = jnp.zeros_like(acc)
    pl.semaphore_wait(barrier, 6)

    @pl.when(core == 0)
    def _():
        for way in range(2):
            z_copy(way, 0, z, 0).start()
            y_copy(way, z, 0).start()

    @pl.when(core == 1)
    def _():
        y_copy(0, z, 1).start()
        y_copy(1, z, 1).start()
        far_copy(z).start()
        y_copy(0, z, 1).wait_recv()
        y_copy(1, z, 1).wait_recv()
        far_copy(z).wait_recv()
        z_copy(0, 0, z, 1).start()
        z_copy(1, 0, z, 1).start()
        sib_copy(z).start()

    def attend(group, masked):
        keys_values = jnp.concatenate(
            [buf[0, group].reshape(NY * BLK, 2 * HD), buf[1, group].reshape(NY * BLK, 2 * HD)], axis=0
        )
        keys = keys_values[:, :HD]
        values = keys_values[:, HD:]
        values = jnp.concatenate([values, jnp.ones_like(values)], axis=1)
        if masked:
            lane = lax.broadcasted_iota(jnp.int32, (BLK, 2 * NY * BLK), 1)
            place = (((lane // BLK) % NY) * 2 + lane // (NY * BLK)) * BLK + lane % BLK
            row = lax.broadcasted_iota(jnp.int32, (BLK, 2 * NY * BLK), 0)
            allowed = place <= (y * 2 + core) * BLK + row
        for head in range(HEADS):
            rows = pl.ds(head * BLK, BLK)
            scores = lax.dot_general(
                q_ref[:, head * HD:(head + 1) * HD], keys, NT, preferred_element_type=F32
            ) * SCORE_SCALE
            if masked:
                scores = jnp.where(allowed, scores, F32(-1e30))
            old = top[rows, :]
            new = jnp.maximum(old, jnp.max(scores, axis=1, keepdims=True))
            top[rows, :] = new
            shrink = jnp.exp2(old - new)
            weights = jnp.exp2(scores - new[:, :1]).astype(BF)
            added = jnp.dot(weights, values, preferred_element_type=F32)
            acc[rows, :] = acc[rows, :] * jnp.concatenate([shrink, shrink], axis=1) + added

    def turn(t, carry):
        step, way = 1 + t // 2, t % 2
        last = 8 - way

        @pl.when(core == 0)
        def _():
            @pl.when(step <= last)
            def _():
                group = group_at(way, step)
                z_copy(way, step, group, 0).wait_recv()

                @pl.when(step < last)
                def _():
                    z_copy(way, step, group, 0).start()

                y_copy(0, group, 0).start()
                y_copy(1, group, 0).start()

            @pl.when((step - 1 <= last) & ((step > 1) | (way == 0)))
            def _():
                group = group_at(way, step - 1)
                y_copy(0, group, 0).wait_recv()
                y_copy(1, group, 0).wait_recv()
                half_copy(0, group).start()
                half_copy(1, group).start()

            @pl.when((step >= 2) & (step - 2 <= last) & ((step > 2) | (way == 0)))
            def _():
                group = group_at(way, step - 2)
                half_copy(0, group).wait_recv()
                half_copy(1, group).wait_recv()
                sib_copy(group).start()

        @pl.when(core == 1)
        def _():
            @pl.when(step <= last)
            def _():
                group = group_at(way, step)
                z_copy(way, step, group, 1).wait_recv()

                @pl.when(step < last)
                def _():
                    z_copy(way, step, group, 1).start()

                sib_copy(group).start()

        @pl.when((step >= 3) & (step - 3 <= last) & ((step > 3) | (way == 0)))
        def _():
            group = group_at(way, step - 3)
            sib_copy(group).wait_recv()

            @pl.when(group == z)
            def _():
                attend(group, True)

            @pl.when(group < z)
            def _():
                attend(group, False)

        return carry

    lax.fori_loop(0, 22, turn, 0)

    for head in range(HEADS):
        rows = slice(head * BLK, (head + 1) * BLK)
        out_ref[:, head * HD:(head + 1) * HD] = (acc[rows, :HD] / acc[rows, HD:]).astype(BF)

    def settle_group(group, carry):
        sib_copy(group).wait_send()

        @pl.when(core == 0)
        def _():
            for way in range(2):
                y_copy(way, group, 0).wait_send()
                half_copy(way, group).wait_send()

        return carry

    def settle_step(step, carry):
        for kind in range(2):
            @pl.when(core == kind)
            def _():
                z_copy(0, step, z, kind).wait_send()

                @pl.when(step < 7)
                def _():
                    z_copy(1, step, z, kind).wait_send()

        return carry

    lax.fori_loop(0, NZ, settle_group, 0)
    lax.fori_loop(0, 8, settle_step, 0)

    @pl.when(core == 1)
    def _():
        y_copy(0, z, 1).wait_send()
        y_copy(1, z, 1).wait_send()
        far_copy(z).wait_send()


def attention(queries, keys_values):
    vmem = pl.BlockSpec(memory_space=pltpu.VMEM)
    dma = pltpu.SemaphoreType.DMA
    return pl.pallas_call(
        attention_kernel,
        out_shape=jax.ShapeDtypeStruct((BLK, HEADS * HD), BF),
        in_specs=[vmem, vmem],
        out_specs=vmem,
        scratch_shapes=[
            pltpu.VMEM((2, NZ, NY, BLK, 2 * HD), BF),
            pltpu.VMEM((HEADS * BLK, HD), F32),
            pltpu.VMEM((HEADS * BLK, 2 * HD), F32),
            dma((2, 9)), dma((NZ,)),
            dma((2, NZ)), dma((2, NZ)),
            dma((2, NZ)), dma((2, NZ)),
            dma((NZ,)), dma((NZ,)),
        ],
        compiler_params=pltpu.CompilerParams(
            collective_id=0, has_side_effects=True, vmem_limit_bytes=40 * 2**20
        ),
        name="gather_attend",
    )(queries, keys_values)


def swap_core(value):
    pairs = []
    for ctx in range(lax.axis_size("ctx")):
        for tp in range(lax.axis_size("tp")):
            xh, core = ctx % 2, tp % 2
            pairs.append((ctx * 4 + tp, (ctx - xh + core) * 4 + tp - core + xh))
    return lax.ppermute(value, ("ctx", "tp"), pairs)


def body(q_text, kv_text, patch_rows, image_count, w_out):
    tok = q_text.shape[0]
    qcols = q_text.shape[1]
    width = patch_rows.shape[1]
    img_rows = patch_rows.shape[0]
    shards = lax.axis_size("ctx")
    me = lax.axis_index("ctx")
    cap = (tok + shards - 1) // shards
    ends = jnp.cumsum(image_count)
    starts = ends - image_count
    row_ids = jnp.arange(img_rows, dtype=jnp.int32)
    image_index = me + shards * row_ids
    target = jnp.sum((ends[None, :] <= image_index[:, None]).astype(jnp.int32), axis=1)
    below = jnp.sum((target[None, :] < target[:, None]).astype(jnp.int32), axis=1)
    slot_of = target * cap + row_ids - below
    placing = (jnp.arange(shards * cap, dtype=jnp.int32)[:, None] == slot_of[None, :]).astype(BF)
    outgoing = jnp.dot(placing, patch_rows, preferred_element_type=F32).astype(BF)
    incoming = lax.all_to_all(
        outgoing.reshape(shards, cap, width), "ctx", split_axis=0, concat_axis=0, tiled=True
    )
    my_count = jnp.take(image_count, me)
    my_start = jnp.take(starts, me)
    local = jnp.arange(tok, dtype=jnp.int32)
    first = tok - my_count
    is_image = local >= first
    index = jnp.clip(my_start + local - first, 0, shards * img_rows - 1)
    source = index % shards
    lowest = (my_start - source + shards - 1) // shards
    pick = source * cap + jnp.clip(index // shards - lowest, 0, cap - 1)
    picked = jnp.take(incoming.reshape(shards * cap, width), pick, axis=0)
    text = jnp.concatenate([q_text, kv_text], axis=1)
    rows = jnp.where(is_image[:, None], picked, text)
    rows = swap_core(rows)
    attended = attention(rows[:, :qcols], rows[:, qcols:])
    attended = swap_core(attended)
    partial_sums = jnp.dot(
        attended,
        lax.all_gather(w_out, "ctx", axis=0, tiled=True),
        preferred_element_type=F32,
    )
    return lax.psum_scatter(partial_sums.astype(BF), "tp", scatter_dimension=1, tiled=True)


def solution(mesh):
    in_specs = (P("ctx", "tp"), P("ctx", "tp"), P("ctx", "tp"), P(), P(("tp", "ctx"), None))
    out_specs = P("ctx", "tp")
    return jax.shard_map(body, mesh=mesh, in_specs=in_specs, out_specs=out_specs, check_vma=False)
```

time: 598 us -> 306 us (0.51)
  waiting for transfers between devices: 377 us -> 177 us
  matrix products: 61.1 us -> 4.16 us
  Pallas kernels: 0 us -> 53.9 us
  starting transfers between devices: 83.8 us -> 35.8 us
  other arithmetic: 34.3 us -> 2.33 us
  local copies, waits for them, and re-layouts: 24.2 us -> 17.7 us
    all_gather x1 -> x0, waiting for transfers between devices: 182 us -> none  [body(): piece = lax.all_gather(key_value, 'ctx', axis=0, tiled=True)]
    dot_general x5 -> x1, matrix products: 57.1 us -> 0.22 us  [body(): jnp.dot(placing, patch_rows, preferred_element_type=F32).astype(BF)]
    pallas_call x0 -> x1, Pallas kernels: none -> 53.9 us  [attention(): pl.pallas_call(attention_kernel, out_shape=jax.ShapeDtypeStruct((BLK, HEA...]
    ppermute x14 -> x2, starting transfers between devices: 60.7 us -> 12.8 us  [swap_core(): return lax.ppermute(value, ('ctx', 'tp'), pairs)]
    ppermute x14 -> x2, waiting for transfers between devices: 50.7 us -> 4.39 us  [swap_core(): return lax.ppermute(value, ('ctx', 'tp'), pairs)]
    reduce_sum x2 -> x0, other arithmetic: 28.9 us -> none  [half_step(): total = jnp.sum(expo, axis=-1)]
    all_gather x1, waiting for transfers between devices: 96.4 us -> 125 us  [body(): lax.all_gather(w_out, 'ctx', axis=0, tiled=True)]
    slice x6 -> x2, local copies, waits for them, and re-layouts: 6.63 us -> 0.02 us  [body(): attended = attention(rows[:, :qcols], rows[:, qcols:])]
  transfers between devices with their start and end apart: 18 -> 5, of which waited for: 16 -> 4; matrix products, arithmetic and copies ran while one was open for 18% -> 6% of each run, Pallas kernels for 0% -> 18%
where the time goes in v1:
time: 306 us
  waiting for transfers between devices  177 us (58%)
  Pallas kernels  53.9 us (18%)
  starting transfers between devices  35.8 us (12%)
  local copies, waits for them, and re-layouts  17.7 us (6%)
  between operations  14.8 us (5%)
  matrix products  4.16 us (1%)
    all_gather x1, waiting for transfers between devices, body(): lax.all_gather(w_out, 'ctx', axis=0, tiled=True)  125 us
    pallas_call x1, Pallas kernels, attention(): pl.pallas_call(attention_kernel, out_shape=jax.ShapeDtypeStruct((BLK, HEA...  53.9 us
    unnamed x3, waiting for transfers between devices  31.5 us
    all_to_all x1, starting transfers between devices, body(): lax.all_to_all(outgoing.reshape(shards, cap, width), 'ctx', split_axis=0,...  23 us
    all_to_all x1, waiting for transfers between devices, body(): lax.all_to_all(outgoing.reshape(shards, cap, width), 'ctx', split_axis=0,...  16.1 us
    unnamed x12, local copies, waits for them, and re-layouts  13.5 us
    ppermute x2, starting transfers between devices, swap_core(): return lax.ppermute(value, ('ctx', 'tp'), pairs)  12.8 us
  transfers between devices with their start and end apart: 5, of which 4 were waited for; matrix products, arithmetic and copies ran while one was open for 6% of the time, Pallas kernels for 18%

profile of v1, /device:TPU:1, one launch (start us, length us, event | category | flops | bytes accessed | tf_op | source)
XLA Modules:
  0.0 305.6 jit_solution(9014292835414044945)
XLA Ops:
  6.5 0.7 all-gather.3.cloned.1.call-update
  7.3 0.8 copy.12
  8.0 0.2 reduce-window.8
  8.2 0.1 reduce
  8.3 0.2 convert_reduce_fusion.1
  8.5 0.2 convert_reduce_fusion
  8.7 0.2 fusion
  8.9 0.5 broadcast.309
  9.4 0.8 reduce.1
  10.2 1.1 reshape.275
  11.3 23.0 %all-to-all-start = ((bf16[128,2,576]{2,1,0:T(2,128)(2,1)}), bf16[128,2,576]{2,1,0:T(2,128)(2,1)S(1)}, u32[]{:S(2)}, u32[]{:S(2)}) async-start(bf16[128,2,576]{2,1,0:T(2,128)(2,1)} %reshape.275), calls=%async_computation | async-start | bytes 655360 | tf_op jit(solution)/shard_map/all_to_all | solution.py:273
  34.2 0.0 reduce-scatter.4.cloned.1.call-start
  34.3 1.3 dynamic-slice.4
  35.6 0.7 sub.78
  36.3 0.6 dynamic-slice.5
  38.2 16.1 %all-to-all-done = bf16[128,2,576]{2,1,0:T(2,128)(2,1)S(1)} async-done(((bf16[128,2,576]{2,1,0:T(2,128)(2,1)}), bf16[128,2,576]{2,1,0:T(2,128)(2,1)S(1)}, u32[]{:S(2)}, u32[]{:S(2)}) %all-to-all-start) | async-done | bytes 294944 | tf_op jit(solution)/shard_map/all_to_all | solution.py:273
  54.3 0.5 reshape.276
  54.9 0.9 gather_fusion
  55.8 0.0 copy-done.2
  55.8 0.2 maximum_select_fusion
  56.0 8.2 %collective-permute-start = (bf16[128,1152]{1,0:T(8,128)(2,1)S(1)}, bf16[128,1152]{1,0:T(8,128)(2,1)S(1)}, u32[]{:S(2)}, u32[]{:S(2)}) collective-permute-start(bf16[128,1152]{1,0:T(8,128)(2,1)S(1)} %maximum_select_fusion), channel_id=1, source_target_pairs={{0,0},{1,4},{2,2},{3,6},{4,1},{5,5},{6,3},{7,7},{8,8},{9,12},{10,1... | collective-permute-start | bytes 884744 | tf_op jit(solution)/shard_map/ppermute | solution.py:253
  64.2 4.4 %collective-permute-done = bf16[128,1152]{1,0:T(8,128)(2,1)S(1)} collective-permute-done((bf16[128,1152]{1,0:T(8,128)(2,1)S(1)}, bf16[128,1152]{1,0:T(8,128)(2,1)S(1)}, u32[]{:S(2)}, u32[]{:S(2)}) %collective-permute-start) | collective-permute-done | bytes 294944 | tf_op jit(solution)/shard_map/ppermute | solution.py:253
  68.6 53.9 %gather_attend.1 = bf16[128,896]{1,0:T(8,128)(2,1)S(1)} custom-call(bf16[128,896]{1,0:T(8,128)(2,1)S(1)} %slice.20.q_ref, bf16[128,256]{1,0:T(8,128)(2,1)S(1)} %slice.21.kv_ref), custom_call_target="tpu_custom_call" | custom-call | tf_op jit(solution)/shard_map/gather_attend/pallas_call | solution.py:226
  122.6 4.6 %collective-permute-start.1 = (bf16[128,896]{1,0:T(8,128)(2,1)S(1)}, bf16[128,896]{1,0:T(8,128)(2,1)S(1)}, u32[]{:S(2)}, u32[]{:S(2)}) collective-permute-start(bf16[128,896]{1,0:T(8,128)(2,1)S(1)} %gather_attend.1), channel_id=1, source_target_pairs={{0,0},{1,4},{2,2},{3,6},{4,1},{5,5},{6,3},{7,7},{8,8},{9,12},{10,1... | collective-permute-start | bytes 688136 | tf_op jit(solution)/shard_map/ppermute | solution.py:253
  127.2 124.9 %all-gather.3.cloned.1.call-done = bf16[128,7,3584]{2,1,0:T(8,128)(2,1)} async-done(((bf16[1,7,3584]{2,1,0:T(8,128)(2,1)}), bf16[128,7,3584]{2,1,0:T(8,128)(2,1)}) %all-gather.3.cloned.1.call-update) | async-done | bytes 6422544 | tf_op jit(solution)/shard_map/all_gather | solution.py:293
  252.0 8.9 %reshape.271 = bf16[896,3584]{1,0:T(8,128)(2,1)} reshape(bf16[128,7,3584]{2,1,0:T(8,128)(2,1)} %all-gather.3.cloned.1.call-done) | data formatting | bytes 12845056
  260.9 0.0 collective-permute-done.1
  260.9 3.9 %convolution_convert_fusion = bf16[128,3584]{1,0:T(8,128)(2,1)S(1)} fusion(bf16[128,896]{1,0:T(8,128)(2,1)S(1)} %collective-permute-done.1, bf16[896,3584]{1,0:T(8,128)(2,1)} %reshape.271), kind=kOutput, calls=%fused_computation.1 | convolution fusion | flops 822542336 | bytes 7569408 | tf_op jit(solution)/shard_map/dot_general | solution.py:291
  264.9 1.3 copy.14
  266.2 0.0 reduce-scatter.4.cloned.1.call-update
  266.2 30.8 %reduce-scatter.4.cloned.1.call-done = bf16[896,128]{1,0:T(8,128)(2,1)} async-done(((bf16[3584,128]{1,0:T(8,128)(2,1)}), bf16[896,128]{1,0:T(8,128)(2,1)}) %reduce-scatter.4.cloned.1.call-update) | async-done | bytes 229392
  297.0 1.8 copy.15
  (14 shorter events, 0.2 us)
Async XLA Ops:
  6.5 2.2 copy-start
  6.5 49.2 %copy-start.2 = (bf16[128,256]{1,0:T(8,128)(2,1)S(1)}, bf16[128,256]{1,0:T(8,128)(2,1)}, u32[]{:S(2)}) copy-start(bf16[128,256]{1,0:T(8,128)(2,1)} %param.6) | copy-start | bytes 196612
  6.5 49.2 %copy-start.1 = (bf16[128,896]{1,0:T(8,128)(2,1)S(1)}, bf16[128,896]{1,0:T(8,128)(2,1)}, u32[]{:S(2)}) copy-start(bf16[128,896]{1,0:T(8,128)(2,1)} %param.5) | copy-start | bytes 688132
  6.5 245.5 %all-gather.3.cloned.1.call-start = ((), (), s32[]{:S(2)}) async-start(), calls=%async_computation.2 | async-start | bytes 7397376 | tf_op jit(solution)/shard_map/all_gather | solution.py:293
  11.3 43.0 %all-to-all-start = ((bf16[128,2,576]{2,1,0:T(2,128)(2,1)}), bf16[128,2,576]{2,1,0:T(2,128)(2,1)S(1)}, u32[]{:S(2)}, u32[]{:S(2)}) async-start(bf16[128,2,576]{2,1,0:T(2,128)(2,1)} %reshape.275), calls=%async_computation | async-start | bytes 655360 | tf_op jit(solution)/shard_map/all_to_all | solution.py:273
  34.2 262.7 %reduce-scatter.4.cloned.1.call-start = ((), (), s32[]{:S(2)}) async-start(), calls=%async_computation.3 | async-start | bytes 1146880
  56.0 12.6 %collective-permute-start = (bf16[128,1152]{1,0:T(8,128)(2,1)S(1)}, bf16[128,1152]{1,0:T(8,128)(2,1)S(1)}, u32[]{:S(2)}, u32[]{:S(2)}) collective-permute-start(bf16[128,1152]{1,0:T(8,128)(2,1)S(1)} %maximum_select_fusion), channel_id=1, source_target_pairs={{0,0},{1,4},{2,2},{3,6},{4,1},{5,5},{6,3},{7,7},{8,8},{9,12},{10,1... | collective-permute-start | bytes 884744 | tf_op jit(solution)/shard_map/ppermute | solution.py:253
  122.6 138.3 %collective-permute-start.1 = (bf16[128,896]{1,0:T(8,128)(2,1)S(1)}, bf16[128,896]{1,0:T(8,128)(2,1)S(1)}, u32[]{:S(2)}, u32[]{:S(2)}) collective-permute-start(bf16[128,896]{1,0:T(8,128)(2,1)S(1)} %gather_attend.1), channel_id=1, source_target_pairs={{0,0},{1,4},{2,2},{3,6},{4,1},{5,5},{6,3},{7,7},{8,8},{9,12},{10,1... | collective-permute-start | bytes 688136 | tf_op jit(solution)/shard_map/ppermute | solution.py:253
Sparse Core Ops, SparseCore 0:
  11.8 240.1 all-gather.2
  266.3 30.5 reduce-scatter.3

commit v2 on v1

v2 whole, which is shorter than its diff:
```python
import functools

import jax
import jax.numpy as jnp
from jax import lax
from jax.experimental import pallas as pl
from jax.experimental.pallas import tpu as pltpu
from jax.sharding import PartitionSpec as P

HD = 128
HEADS = 7
BLK = 128
NZ, NY = 16, 4
BF = jnp.bfloat16
F32 = jnp.float32
NT = (((1,), (1,)), ((), ()))
SCORE_SCALE = 0.08838834764831845 * 1.4426950408889634
MESH = pl.DeviceIdType.MESH
VMEM = pl.BlockSpec(memory_space=pltpu.VMEM)
DMA = pltpu.SemaphoreType.DMA


class Place:
    def __init__(self):
        ctx = lax.axis_index("ctx")
        tp = lax.axis_index("tp")
        self.z, self.y, self.xh = ctx // 8, (ctx // 2) % 4, ctx % 2
        self.xl, self.core = tp // 2, tp % 2
        self.x = self.xh * 2 + self.xl

    def device(self, z=None, y=None, x=None, core=None):
        z = self.z if z is None else z
        y = self.y if y is None else y
        x = self.x if x is None else x
        core = self.core if core is None else core
        return ((z * 4 + y) * 2 + x // 2, (x % 2) * 2 + core)

    def copy(self, src, dst, send, recv, **where):
        return pltpu.make_async_remote_copy(
            src_ref=src, dst_ref=dst, send_sem=send, recv_sem=recv,
            device_id=self.device(**where), device_id_type=MESH,
        )

    def greet(self, wheres):
        barrier = pltpu.get_barrier_semaphore()
        for where in wheres:
            pl.semaphore_signal(
                barrier, inc=1, device_id=self.device(**where), device_id_type=MESH
            )
        return barrier

    def ring_neighbours(self):
        z, y = self.z, self.y
        return [
            dict(z=(z + 1) % NZ), dict(z=(z + NZ - 1) % NZ),
            dict(y=(y + 1) % NY), dict(y=(y + 3) % NY), dict(y=(y + 2) % NY),
            dict(core=1 - self.core),
        ]


SPREAD_SEMS = [
    DMA((2, 9)), DMA((NZ,)), DMA((2, NZ)), DMA((2, NZ)), DMA((2, NZ)), DMA((2, NZ)),
    DMA((NZ,)), DMA((NZ,)),
]


class Spread:
    def __init__(self, place, buf, sems, half):
        self.p, self.buf, self.half = place, buf, half
        (self.z_send, self.z_recv, self.y_send, self.y_recv,
         self.h_send, self.h_recv, self.sib_send, self.sib_recv) = sems

    def z_copy(self, way, step, group, kind):
        p = self.p
        part = self.buf.at[0, group, p.y] if kind == 0 else self.buf.at[1, group]
        return p.copy(part, part, self.z_send.at[way, step], self.z_recv.at[group],
                      z=(p.z + 17 - 2 * way) % NZ)

    def y_copy(self, way, group, kind):
        p = self.p
        part = self.buf.at[kind, group, p.y]
        return p.copy(part, part, self.y_send.at[way, group], self.y_recv.at[way, group],
                      y=(p.y + 1 + 2 * way) % NY)

    def far_copy(self, group):
        p = self.p
        part = self.buf.at[1, group, p.y]
        return p.copy(part, part, self.h_send.at[0, group], self.h_recv.at[0, group],
                      y=(p.y + 2) % NY)

    def half_copy(self, way, group):
        p = self.p
        part = self.half(self.buf.at[0, group, (p.y + 3 + 2 * way) % NY], way)
        return p.copy(part, part, self.h_send.at[way, group], self.h_recv.at[way, group],
                      y=(p.y + 1 + 2 * way) % NY)

    def sib_copy(self, group):
        p = self.p
        part = self.buf.at[p.core, group]
        return p.copy(part, part, self.sib_send.at[group], self.sib_recv.at[group],
                      core=1 - p.core)

    def group_at(self, way, step):
        return (self.p.z + NZ - step + 2 * step * way) % NZ

    def begin(self):
        p = self.p

        @pl.when(p.core == 0)
        def _():
            for way in range(2):
                self.z_copy(way, 0, p.z, 0).start()
                self.y_copy(way, p.z, 0).start()

        @pl.when(p.core == 1)
        def _():
            first = [self.y_copy(0, p.z, 1), self.y_copy(1, p.z, 1), self.far_copy(p.z)]
            for copy in first:
                copy.start()
            for copy in first:
                copy.wait_recv()
            self.z_copy(0, 0, p.z, 1).start()
            self.z_copy(1, 0, p.z, 1).start()
            self.sib_copy(p.z).start()

    def advance(self, step, way):
        p = self.p
        last = 8 - way

        @pl.when(p.core == 0)
        def _():
            @pl.when(step <= last)
            def _():
                group = self.group_at(way, step)
                self.z_copy(way, step, group, 0).wait_recv()

                @pl.when(step < last)
                def _():
                    self.z_copy(way, step, group, 0).start()

                self.y_copy(0, group, 0).start()
                self.y_copy(1, group, 0).start()

            @pl.when((step - 1 <= last) & ((step > 1) | (way == 0)))
            def _():
                group = self.group_at(way, step - 1)
                self.y_copy(0, group, 0).wait_recv()
                self.y_copy(1, group, 0).wait_recv()
                self.half_copy(0, group).start()
                self.half_copy(1, group).start()

            @pl.when((step >= 2) & (step - 2 <= last) & ((step > 2) | (way == 0)))
            def _():
                group = self.group_at(way, step - 2)
                self.half_copy(0, group).wait_recv()
                self.half_copy(1, group).wait_recv()
                self.sib_copy(group).start()

        @pl.when(p.core == 1)
        def _():
            @pl.when(step <= last)
            def _():
                group = self.group_at(way, step)
                self.z_copy(way, step, group, 1).wait_recv()

                @pl.when(step < last)
                def _():
                    self.z_copy(way, step, group, 1).start()

                self.sib_copy(group).start()

    def arrived(self, step, way, then):
        @pl.when((step >= 3) & (step - 3 <= 8 - way) & ((step > 3) | (way == 0)))
        def _():
            group = self.group_at(way, step - 3)
            self.sib_copy(group).wait_recv()
            if then is not None:
                then(group)

    def settle(self):
        p = self.p

        def settle_group(group, carry):
            self.sib_copy(group).wait_send()

            @pl.when(p.core == 0)
            def _():
                for way in range(2):
                    self.y_copy(way, group, 0).wait_send()
                    self.half_copy(way, group).wait_send()

            return carry

        def settle_step(step, carry):
            for kind in range(2):
                @pl.when(p.core == kind)
                def _():
                    self.z_copy(0, step, p.z, kind).wait_send()

                    @pl.when(step < 7)
                    def _():
                        self.z_copy(1, step, p.z, kind).wait_send()

            return carry

        lax.fori_loop(0, NZ, settle_group, 0)
        lax.fori_loop(0, 8, settle_step, 0)

        @pl.when(p.core == 1)
        def _():
            self.y_copy(0, p.z, 1).wait_send()
            self.y_copy(1, p.z, 1).wait_send()
            self.far_copy(p.z).wait_send()


def attention_kernel(q_ref, kv_ref, out_ref, buf, top, acc, *sems):
    p = Place()
    spread = Spread(p, buf, sems, lambda block, way: block.at[pl.ds(way * 64, 64)])
    barrier = p.greet(p.ring_neighbours())
    buf[p.core, p.z, p.y] = kv_ref[...]
    top[...] = jnp.full_like(top, -1e30)
    acc[...] = jnp.zeros_like(acc)
    pl.semaphore_wait(barrier, 6)
    spread.begin()

    def attend(group, masked):
        keys_values = jnp.concatenate(
            [buf[0, group].reshape(NY * BLK, 2 * HD), buf[1, group].reshape(NY * BLK, 2 * HD)], axis=0
        )
        keys = keys_values[:, :HD]
        values = keys_values[:, HD:]
        values = jnp.concatenate([values, jnp.ones_like(values)], axis=1)
        if masked:
            lane = lax.broadcasted_iota(jnp.int32, (BLK, 2 * NY * BLK), 1)
            position = (((lane // BLK) % NY) * 2 + lane // (NY * BLK)) * BLK + lane % BLK
            row = lax.broadcasted_iota(jnp.int32, (BLK, 2 * NY * BLK), 0)
            allowed = position <= (p.y * 2 + p.core) * BLK + row
        for head in range(HEADS):
            rows = pl.ds(head * BLK, BLK)
            scores = lax.dot_general(
                q_ref[:, head * HD:(head + 1) * HD], keys, NT, preferred_element_type=F32
            ) * SCORE_SCALE
            if masked:
                scores = jnp.where(allowed, scores, F32(-1e30))
            old = top[rows, :]
            new = jnp.maximum(old, jnp.max(scores, axis=1, keepdims=True))
            top[rows, :] = new
            shrink = jnp.exp2(old - new)
            weights = jnp.exp2(scores - new[:, :1]).astype(BF)
            added = jnp.dot(weights, values, preferred_element_type=F32)
            acc[rows, :] = acc[rows, :] * jnp.concatenate([shrink, shrink], axis=1) + added

    def attend_any(group):
        @pl.when(group == p.z)
        def _():
            attend(group, True)

        @pl.when(group < p.z)
        def _():
            attend(group, False)

    def turn(t, carry):
        step, way = 1 + t // 2, t % 2
        spread.advance(step, way)
        spread.arrived(step, way, attend_any)
        return carry

    lax.fori_loop(0, 22, turn, 0)
    for head in range(HEADS):
        rows = slice(head * BLK, (head + 1) * BLK)
        out_ref[:, head * HD:(head + 1) * HD] = (acc[rows, :HD] / acc[rows, HD:]).astype(BF)
    spread.settle()


def attention(queries, keys_values):
    return pl.pallas_call(
        attention_kernel,
        out_shape=jax.ShapeDtypeStruct((BLK, HEADS * HD), BF),
        in_specs=[VMEM, VMEM],
        out_specs=VMEM,
        scratch_shapes=[
            pltpu.VMEM((2, NZ, NY, BLK, 2 * HD), BF),
            pltpu.VMEM((HEADS * BLK, HD), F32),
            pltpu.VMEM((HEADS * BLK, 2 * HD), F32),
            *SPREAD_SEMS,
        ],
        compiler_params=pltpu.CompilerParams(
            collective_id=0, has_side_effects=True, vmem_limit_bytes=40 * 2**20
        ),
        name="gather_attend",
    )(queries, keys_values)


QCOLS = HEADS * HD
PIECE = 16


def weight_kernel(piece_ref, w_ref, pieces, x_send, x_recv, own_sem, merged, *sems):
    p = Place()
    spread = Spread(p, w_ref, sems, lambda block, way: block.at[way])
    barrier = p.greet(p.ring_neighbours() + [dict(x=(p.x + j) % 4) for j in (1, 2, 3)])
    pl.semaphore_wait(barrier, 9)

    def columns(x):
        return (x % 2) * 2 + x // 2

    def x_copy(j):
        x = (p.x + j) % 4
        return p.copy(piece_ref.at[columns(x)], pieces.at[p.x], x_send.at[j - 1], x_recv.at[j - 1],
                      x=x)

    def x_arrival(j):
        x = (p.x + 4 - j) % 4
        return p.copy(pieces.at[x], pieces.at[x], x_send.at[j - 1], x_recv.at[j - 1], x=x)

    for j in (1, 2, 3):
        x_copy(j).start()
    pieces[p.x] = piece_ref[columns(p.x)]
    for j in (1, 2, 3):
        x_arrival(j).wait_recv()
    for xl in range(2):
        merged[xl] = pieces[xl] + pieces[2 + xl]
    own = pltpu.make_async_copy(merged, w_ref.at[p.core, p.z, p.y], own_sem)
    own.start()
    own.wait()
    spread.begin()

    def turn(t, carry):
        step, way = 1 + t // 2, t % 2
        spread.advance(step, way)
        spread.arrived(step, way, None)
        return carry

    lax.fori_loop(0, 22, turn, 0)
    for j in (1, 2, 3):
        x_copy(j).wait_send()
    spread.settle()


def gather_weights(w_out):
    xh = lax.axis_index("ctx") % 2
    rows = w_out.shape[0]
    piece = jnp.where(
        xh == 0,
        jnp.pad(w_out, ((0, PIECE - rows), (0, 0))),
        jnp.pad(w_out, ((rows, PIECE - 2 * rows), (0, 0))),
    )
    piece = jnp.transpose(piece.reshape(PIECE, 4, QCOLS), (1, 0, 2))
    return pl.pallas_call(
        weight_kernel,
        out_shape=jax.ShapeDtypeStruct((2, NZ, NY, 2, PIECE, QCOLS), BF),
        in_specs=[VMEM],
        out_specs=pl.BlockSpec(memory_space=pl.ANY),
        scratch_shapes=[
            pltpu.VMEM((4, PIECE, QCOLS), BF), DMA((3,)), DMA((3,)), DMA,
            pltpu.VMEM((2, PIECE, QCOLS), BF),
            *SPREAD_SEMS,
        ],
        compiler_params=pltpu.CompilerParams(
            collective_id=1, has_side_effects=True, vmem_limit_bytes=16 * 2**20
        ),
        name="gather_weights",
    )(piece)


def project_kernel(
    att_ref, w_ref, out_ref, w, heads,
    w_sem, x_send, x_recv, h_send, h_recv,
):
    p = Place()
    x_up, x_down, x_far = (p.x + 1) % 4, (p.x + 3) % 4, (p.x + 2) % 4
    depth = NZ * NY * PIECE
    half = BLK // 2
    barrier = p.greet([dict(x=x_up), dict(x=x_down)])
    fetch = pltpu.make_async_copy(w_ref, w, w_sem)
    fetch.start()
    row = lax.broadcasted_iota(jnp.int32, (QCOLS, depth), 0)
    lane = lax.broadcasted_iota(jnp.int32, (QCOLS, depth), 1)
    spot = (lane // PIECE) * (PIECE - 2) + lane % PIECE
    widen = ((row == spot) & (lane % PIECE < PIECE - 2)).astype(F32).astype(BF)
    heads[p.x] = jnp.dot(att_ref[...], widen, preferred_element_type=F32).astype(BF)
    pl.semaphore_wait(barrier, 2)


    def block_copy(way):
        part = heads.at[p.x]
        return p.copy(part, part, x_send.at[way], x_recv.at[way], x=(p.x + 1 + 2 * way) % 4)

    def half_copy(way):
        part = heads.at[(p.x + 3 + 2 * way) % 4, pl.ds(way * half, half)]
        return p.copy(part, part, h_send.at[way], h_recv.at[way], x=(p.x + 1 + 2 * way) % 4)

    def product(x):
        group_xh, group_xl = x // 2, x % 2
        rows = w[group_xh, :, :, group_xl].reshape(depth, QCOLS)
        return jnp.dot(heads[x], rows, preferred_element_type=F32)

    block_copy(0).start()
    block_copy(1).start()
    fetch.wait()
    total = product(p.x)
    block_copy(0).wait_recv()
    half_copy(0).start()
    block_copy(1).wait_recv()
    half_copy(1).start()
    total += product(x_down)
    total += product(x_up)
    half_copy(0).wait_recv()
    half_copy(1).wait_recv()
    total += product(x_far)
    out_ref[...] = total.astype(BF)
    for way in range(2):
        block_copy(way).wait_send()
        half_copy(way).wait_send()


def project(attended, weights):
    return pl.pallas_call(
        project_kernel,
        out_shape=jax.ShapeDtypeStruct((BLK, QCOLS), BF),
        in_specs=[VMEM, pl.BlockSpec(memory_space=pl.ANY)],
        out_specs=VMEM,
        scratch_shapes=[
            pltpu.VMEM((2, NZ, NY, 2, PIECE, QCOLS), BF),
            pltpu.VMEM((4, BLK, NZ * NY * PIECE), BF),

            DMA, DMA((2,)), DMA((2,)), DMA((2,)), DMA((2,)),
        ],
        compiler_params=pltpu.CompilerParams(
            collective_id=2, has_side_effects=True, vmem_limit_bytes=48 * 2**20
        ),
        name="project",
    )(attended, weights)


def swap_core(value):
    pairs = []
    for ctx in range(lax.axis_size("ctx")):
        for tp in range(lax.axis_size("tp")):
            xh, core = ctx % 2, tp % 2
            pairs.append((ctx * 4 + tp, (ctx - xh + core) * 4 + tp - core + xh))
    return lax.ppermute(value, ("ctx", "tp"), pairs)


def body(q_text, kv_text, patch_rows, image_count, w_out):
    weights = gather_weights(w_out)
    tok = q_text.shape[0]
    qcols = q_text.shape[1]
    width = patch_rows.shape[1]
    img_rows = patch_rows.shape[0]
    shards = lax.axis_size("ctx")
    me = lax.axis_index("ctx")
    cap = (tok + shards - 1) // shards
    ends = jnp.cumsum(image_count)
    starts = ends - image_count
    row_ids = jnp.arange(img_rows, dtype=jnp.int32)
    image_index = me + shards * row_ids
    target = jnp.sum((ends[None, :] <= image_index[:, None]).astype(jnp.int32), axis=1)
    below = jnp.sum((target[None, :] < target[:, None]).astype(jnp.int32), axis=1)
    slot_of = target * cap + row_ids - below
    placing = (jnp.arange(shards * cap, dtype=jnp.int32)[:, None] == slot_of[None, :]).astype(BF)
    outgoing = jnp.dot(placing, patch_rows, preferred_element_type=F32).astype(BF)
    incoming = lax.all_to_all(
        outgoing.reshape(shards, cap, width), "ctx", split_axis=0, concat_axis=0, tiled=True
    )
    my_count = jnp.take(image_count, me)
    my_start = jnp.take(starts, me)
    local = jnp.arange(tok, dtype=jnp.int32)
    first = tok - my_count
    is_image = local >= first
    index = jnp.clip(my_start + local - first, 0, shards * img_rows - 1)
    source = index % shards
    lowest = (my_start - source + shards - 1) // shards
    pick = source * cap + jnp.clip(index // shards - lowest, 0, cap - 1)
    picked = jnp.take(incoming.reshape(shards * cap, width), pick, axis=0)
    text = jnp.concatenate([q_text, kv_text], axis=1)
    rows = jnp.where(is_image[:, None], picked, text)
    rows = swap_core(rows)
    attended = attention(rows[:, :qcols], rows[:, qcols:])
    return swap_core(project(attended, weights))


def solution(mesh):
    in_specs = (P("ctx", "tp"), P("ctx", "tp"), P("ctx", "tp"), P(), P(("tp", "ctx"), None))
    out_specs = P("ctx", "tp")
    return jax.shard_map(body, mesh=mesh, in_specs=in_specs, out_specs=out_specs, check_vma=False)
```

time: 306 us -> 190 us (0.62)
  waiting for transfers between devices: 177 us -> 19.7 us
  Pallas kernels: 53.9 us -> 118 us
  between operations: 14.8 us -> 1.43 us
  local copies, waits for them, and re-layouts: 17.7 us -> 9.39 us
  matrix products: 4.16 us -> 0.22 us
    all_gather x1 -> x0, waiting for transfers between devices: 125 us -> none  [body(): lax.all_gather(w_out, 'ctx', axis=0, tiled=True)]
    pallas_call x0 -> x2, Pallas kernels: none -> 63.3 us  [the longest x1 50.8 us: gather_weights(): pl.pallas_call(weight_kernel, out_shape=jax.ShapeDtypeStruct((2, NZ, NY,...]
    unnamed x3 -> x0, waiting for transfers between devices: 31.5 us -> none
    unnamed x12 -> x10, local copies, waits for them, and re-layouts: 13.5 us -> 5.23 us
    dot_general x1 -> x0, matrix products: 3.94 us -> none  [body(): jnp.dot(attended, lax.all_gather(w_out, 'ctx', axis=0, tiled=True), prefe...]
  transfers between devices with their start and end apart: 5 -> 3, of which waited for: 4 -> 2; matrix products, arithmetic and copies ran while one was open for 6% -> 1% of each run, Pallas kernels for 18% -> 27%
where the time goes in v2:
time: 190 us; the launch traced here: 189 us
  Pallas kernels  118 us (62%)
  starting transfers between devices  37.2 us (20%)
  waiting for transfers between devices  19.7 us (10%)
  local copies, waits for them, and re-layouts  9.39 us (5%)
  other arithmetic  3.35 us (2%)
    pallas_call x1, Pallas kernels, attention(): pl.pallas_call(attention_kernel, out_shape=jax.ShapeDtypeStruct((BLK, HEA...  54.9 us
    pallas_call x1, Pallas kernels, gather_weights(): pl.pallas_call(weight_kernel, out_shape=jax.ShapeDtypeStruct((2, NZ, NY,...  50.8 us
    all_to_all x1, starting transfers between devices, body(): lax.all_to_all(outgoing.reshape(shards, cap, width), 'ctx', split_axis=0,...  23 us
    all_to_all x1, waiting for transfers between devices, body(): lax.all_to_all(outgoing.reshape(shards, cap, width), 'ctx', split_axis=0,...  16 us
    ppermute x2, starting transfers between devices, swap_core(): return lax.ppermute(value, ('ctx', 'tp'), pairs)  14.2 us
    pallas_call x1, Pallas kernels, project(): pl.pallas_call(project_kernel, out_shape=jax.ShapeDtypeStruct((BLK, QCOLS...  12.5 us
    unnamed x10, local copies, waits for them, and re-layouts  5.23 us
  transfers between devices with their start and end apart: 3, of which 2 were waited for; matrix products, arithmetic and copies ran while one was open for 1% of the time, Pallas kernels for 27%

profile of v2, /device:TPU:1, one launch (start us, length us, event | category | flops | bytes accessed | tf_op | source)
XLA Modules:
  0.0 189.5 jit_solution(17354366730007941594)
XLA Ops:
  0.0 0.0 copy-start
  0.0 0.0 copy-start.2
  0.0 0.8 copy.15
  0.8 0.2 reduce-window.8
  1.0 0.1 reduce
  1.1 0.2 convert_reduce_fusion.1
  1.3 0.2 convert_reduce_fusion
  1.5 0.0 copy-done
  1.5 0.2 fusion
  1.7 0.5 broadcast.314
  2.2 0.8 reduce.1
  3.0 1.0 reshape.275
  4.0 23.0 %all-to-all-start = ((bf16[128,2,576]{2,1,0:T(2,128)(2,1)}), bf16[128,2,576]{2,1,0:T(2,128)(2,1)S(1)}, u32[]{:S(2)}, u32[]{:S(2)}) async-start(bf16[128,2,576]{2,1,0:T(2,128)(2,1)} %reshape.275), calls=%async_computation | async-start | bytes 655360 | tf_op jit(solution)/shard_map/all_to_all | solution.py:463
  27.0 1.3 dynamic-slice.4
  28.3 0.7 sub.78
  29.0 0.6 dynamic-slice.5
  30.9 16.0 %all-to-all-done = bf16[128,2,576]{2,1,0:T(2,128)(2,1)S(1)} async-done(((bf16[128,2,576]{2,1,0:T(2,128)(2,1)}), bf16[128,2,576]{2,1,0:T(2,128)(2,1)S(1)}, u32[]{:S(2)}, u32[]{:S(2)}) %all-to-all-start) | async-done | bytes 294944 | tf_op jit(solution)/shard_map/all_to_all | solution.py:463
  46.9 0.5 reshape.276
  47.4 0.9 gather_fusion
  48.3 1.2 maximum_select_fusion
  49.5 7.7 %collective-permute-start = (bf16[128,1152]{1,0:T(8,128)(2,1)S(1)}, bf16[128,1152]{1,0:T(8,128)(2,1)S(1)}, u32[]{:S(2)}, u32[]{:S(2)}) collective-permute-start(bf16[128,1152]{1,0:T(8,128)(2,1)S(1)} %maximum_select_fusion), channel_id=1, source_target_pairs={{0,0},{1,4},{2,2},{3,6},{4,1},{5,5},{6,3},{7,7},{8,8},{9,12},{10,1... | collective-permute-start | bytes 884744 | tf_op jit(solution)/shard_map/ppermute | solution.py:442
  57.2 0.0 copy-done.2
  57.3 50.8 %gather_weights.1.w_ref = bf16[2,16,4,2,16,896]{5,4,3,2,1,0:T(8,128)(2,1)S(1)} custom-call(bf16[4,16,896]{2,1,0:T(8,128)(2,1)S(1)} %bitcast.19), custom_call_target="tpu_custom_call" | custom-call | tf_op jit(solution)/shard_map/gather_weights/pallas_call | solution.py:349
  108.1 0.0 copy-start.1
  108.1 3.0 %copy-done.1 = bf16[2,16,4,2,16,896]{5,4,3,2,1,0:T(8,128)(2,1)} copy-done((bf16[2,16,4,2,16,896]{5,4,3,2,1,0:T(8,128)(2,1)}, bf16[2,16,4,2,16,896]{5,4,3,2,1,0:T(8,128)(2,1)S(1)}, u32[]{:S(2)}) %copy-start.1) | copy-done | bytes 7340056
  111.1 0.0 collective-permute-done
  111.1 54.9 %gather_attend.1.att_ref = bf16[128,896]{1,0:T(8,128)(2,1)S(1)} custom-call(bf16[128,896]{1,0:T(8,128)(2,1)S(1)} %slice.20.q_ref, bf16[128,256]{1,0:T(8,128)(2,1)S(1)} %slice.21.kv_ref), custom_call_target="tpu_custom_call" | custom-call | tf_op jit(solution)/shard_map/gather_attend/pallas_call | solution.py:276
  166.0 12.5 %project.1 = bf16[128,896]{1,0:T(8,128)(2,1)S(1)} custom-call(bf16[128,896]{1,0:T(8,128)(2,1)S(1)} %gather_attend.1.att_ref, bf16[2,16,4,2,16,896]{5,4,3,2,1,0:T(8,128)(2,1)} %copy-done.1), custom_call_target="tpu_custom_call" | custom-call | tf_op jit(solution)/shard_map/project/pallas_call | solution.py:418
  178.5 6.5 %collective-permute-start.1 = (bf16[128,896]{1,0:T(8,128)(2,1)S(1)}, bf16[128,896]{1,0:T(8,128)(2,1)S(1)}, u32[]{:S(2)}, u32[]{:S(2)}) collective-permute-start(bf16[128,896]{1,0:T(8,128)(2,1)S(1)} %project.1), channel_id=1, source_target_pairs={{0,0},{1,4},{2,2},{3,6},{4,1},{5,5},{6,3},{7,7},{8,8},{9,12},{10,1... | collective-permute-start | bytes 688136 | tf_op jit(solution)/shard_map/ppermute | solution.py:442
  185.1 3.7 %collective-permute-done.1 = bf16[128,896]{1,0:T(8,128)(2,1)S(1)} collective-permute-done((bf16[128,896]{1,0:T(8,128)(2,1)S(1)}, bf16[128,896]{1,0:T(8,128)(2,1)S(1)}, u32[]{:S(2)}, u32[]{:S(2)}) %collective-permute-start.1) | collective-permute-done | bytes 229408 | tf_op jit(solution)/shard_map/ppermute | solution.py:442
  188.8 0.7 copy.26
  (10 shorter events, 0.2 us)
Async XLA Ops:
  0.0 1.5 copy-start
  0.0 57.2 %copy-start.2 = (bf16[7,3584]{1,0:T(8,128)(2,1)S(1)}, bf16[7,3584]{1,0:T(8,128)(2,1)}, u32[]{:S(2)}) copy-start(bf16[7,3584]{1,0:T(8,128)(2,1)} %param.9) | copy-start | bytes 150532
  4.0 42.8 %all-to-all-start = ((bf16[128,2,576]{2,1,0:T(2,128)(2,1)}), bf16[128,2,576]{2,1,0:T(2,128)(2,1)S(1)}, u32[]{:S(2)}, u32[]{:S(2)}) async-start(bf16[128,2,576]{2,1,0:T(2,128)(2,1)} %reshape.275), calls=%async_computation | async-start | bytes 655360 | tf_op jit(solution)/shard_map/all_to_all | solution.py:463
  49.5 61.5 %collective-permute-start = (bf16[128,1152]{1,0:T(8,128)(2,1)S(1)}, bf16[128,1152]{1,0:T(8,128)(2,1)S(1)}, u32[]{:S(2)}, u32[]{:S(2)}) collective-permute-start(bf16[128,1152]{1,0:T(8,128)(2,1)S(1)} %maximum_select_fusion), channel_id=1, source_target_pairs={{0,0},{1,4},{2,2},{3,6},{4,1},{5,5},{6,3},{7,7},{8,8},{9,12},{10,1... | collective-permute-start | bytes 884744 | tf_op jit(solution)/shard_map/ppermute | solution.py:442
  108.1 3.0 %copy-start.1 = (bf16[2,16,4,2,16,896]{5,4,3,2,1,0:T(8,128)(2,1)}, bf16[2,16,4,2,16,896]{5,4,3,2,1,0:T(8,128)(2,1)S(1)}, u32[]{:S(2)}) copy-start(bf16[2,16,4,2,16,896]{5,4,3,2,1,0:T(8,128)(2,1)S(1)} %gather_weights.1.w_ref) | copy-start | bytes 22020100
  178.5 10.2 %collective-permute-start.1 = (bf16[128,896]{1,0:T(8,128)(2,1)S(1)}, bf16[128,896]{1,0:T(8,128)(2,1)S(1)}, u32[]{:S(2)}, u32[]{:S(2)}) collective-permute-start(bf16[128,896]{1,0:T(8,128)(2,1)S(1)} %project.1), channel_id=1, source_target_pairs={{0,0},{1,4},{2,2},{3,6},{4,1},{5,5},{6,3},{7,7},{8,8},{9,12},{10,1... | collective-permute-start | bytes 688136 | tf_op jit(solution)/shard_map/ppermute | solution.py:442

commit v3 on v0

v3 whole, which is shorter than its diff:
```python
import functools

import jax
import jax.numpy as jnp
from jax import lax
from jax.experimental import pallas as pl
from jax.experimental.pallas import tpu as pltpu
from jax.sharding import PartitionSpec as P

HD = 128
HEADS = 7
BLK = 128
NZ, NY = 16, 4
BF = jnp.bfloat16
F32 = jnp.float32
NT = (((1,), (1,)), ((), ()))
SCORE_SCALE = 0.08838834764831845 * 1.4426950408889634
MESH = pl.DeviceIdType.MESH
VMEM = pl.BlockSpec(memory_space=pltpu.VMEM)
DMA = pltpu.SemaphoreType.DMA


class Place:
    def __init__(self):
        ctx = lax.axis_index("ctx")
        tp = lax.axis_index("tp")
        self.z, self.y, self.xh = ctx // 8, (ctx // 2) % 4, ctx % 2
        self.xl, self.core = tp // 2, tp % 2
        self.x = self.xh * 2 + self.xl

    def device(self, z=None, y=None, x=None, core=None):
        z = self.z if z is None else z
        y = self.y if y is None else y
        x = self.x if x is None else x
        core = self.core if core is None else core
        return ((z * 4 + y) * 2 + x // 2, (x % 2) * 2 + core)

    def copy(self, src, dst, send, recv, **where):
        return pltpu.make_async_remote_copy(
            src_ref=src, dst_ref=dst, send_sem=send, recv_sem=recv,
            device_id=self.device(**where), device_id_type=MESH,
        )

    def greet(self, wheres):
        barrier = pltpu.get_barrier_semaphore()
        for where in wheres:
            pl.semaphore_signal(
                barrier, inc=1, device_id=self.device(**where), device_id_type=MESH
            )
        return barrier

    def ring_neighbours(self):
        z, y = self.z, self.y
        return [
            dict(z=(z + 1) % NZ), dict(z=(z + NZ - 1) % NZ),
            dict(y=(y + 1) % NY), dict(y=(y + 3) % NY), dict(y=(y + 2) % NY),
            dict(core=1 - self.core),
        ]


QCOLS = HEADS * HD
PIECE = 16
STEPS = 9
TURNS = 12
SPREAD_SEMS = [
    DMA((2,)), DMA((2,)), DMA((3,)), DMA((3,)), DMA((3,)), DMA((3,)),
    DMA((2, STEPS)), DMA((2, STEPS)), DMA((2, STEPS)), DMA((2, STEPS)),
    DMA((2, STEPS)), DMA((2, STEPS)), DMA((2, STEPS)), DMA((2, STEPS)),
]


class Spread:
    def __init__(self, place, one, row, half, sems):
        self.p, self.one, self.row, self.half = place, one, row, half
        (self.w_send, self.w_recv, self.f_send, self.f_recv, self.o_send, self.o_recv,
         self.z_send, self.z_recv,
         self.y_send, self.y_recv, self.h_send, self.h_recv, self.s_send, self.s_recv) = sems
        self.last = 8 - place.core

    def group(self, way, step):
        return (self.p.z + NZ - step + 2 * step * way) % NZ

    def waits(self, ref, sem):
        self.p.copy(ref, ref, self.w_send.at[0], sem, core=1 - self.p.core).wait_recv()

    def z_part(self, part, step):
        p, group = self.p, self.group(self.p.core, step)
        return self.one(0, group, p.y) if part == 0 else self.row(1, group)

    def z_copy(self, part, step):
        p, ref = self.p, self.z_part(part, step)
        return p.copy(ref, ref, self.z_send.at[part, step], self.z_recv.at[part, step + 1],
                      z=(p.z + 17 - 2 * p.core) % NZ)

    def y_copy(self, way, step):
        p = self.p
        ref = self.one(0, self.group(p.core, step), p.y)
        return p.copy(ref, ref, self.y_send.at[way, step], self.y_recv.at[way, step],
                      y=(p.y + 1 + 2 * way) % NY)

    def half_copy(self, way, step):
        p = self.p
        ref = self.half(self.one(0, self.group(p.core, step), (p.y + 3 + 2 * way) % NY), way)
        return p.copy(ref, ref, self.h_send.at[way, step], self.h_recv.at[way, step],
                      y=(p.y + 1 + 2 * way) % NY)

    def first_copy(self, j):
        p, ref = self.p, self.one(1, self.p.z, self.p.y)
        return p.copy(ref, ref, self.f_send.at[j], self.f_recv.at[j], y=(p.y + 1 + j) % NY)

    def sib_copy(self, part, step):
        p = self.p
        ref = self.row(part, self.group(p.core, step))
        return p.copy(ref, ref, self.s_send.at[part, step], self.s_recv.at[part, step],
                      core=1 - p.core)

    def own_copy(self, j):
        p = self.p
        ref = self.one(0, p.z, (p.y + 1 + j) % NY)
        return p.copy(ref, ref, self.o_send.at[j], self.o_recv.at[j], core=1 - p.core)

    def begin(self):
        self.z_copy(0, 0).start()
        for j in range(3):
            self.first_copy(j).start()

        @pl.when(self.p.core == 0)
        def _():
            self.y_copy(0, 0).start()
            self.y_copy(1, 0).start()

    def begin_b(self):
        for j in range(3):
            self.first_copy(j).wait_recv()
        self.z_copy(1, 0).start()

    def along_z(self, step):
        for part in range(2):
            @pl.when(step <= self.last)
            def _():
                self.waits(self.z_part(part, step), self.z_recv.at[part, step])

                @pl.when(step < self.last)
                def _():
                    self.z_copy(part, step).start()

                if part == 0:
                    self.y_copy(0, step).start()
                    self.y_copy(1, step).start()
                else:
                    self.sib_copy(1, step).start()

    def along_y(self, step):
        core = self.p.core

        @pl.when((step - 1 <= self.last) & (step - 1 >= core))
        def _():
            for way in range(2):
                self.y_copy(way, step - 1).wait_recv()
                self.half_copy(way, step - 1).start()

        @pl.when((step - 2 <= self.last) & (step - 2 >= core))
        def _():
            for way in range(2):
                self.half_copy(way, step - 2).wait_recv()

            @pl.when(step > 2)
            def _():
                self.sib_copy(0, step - 2).start()

            @pl.when(step == 2)
            def _():
                for j in range(3):
                    self.own_copy(j).start()

    def own_arrived(self):
        @pl.when(self.p.core == 1)
        def _():
            for j in range(3):
                self.own_copy(j).wait_recv()

    def sib_arrived(self, step):
        group = self.group(1 - self.p.core, step)
        for part in range(2):
            self.waits(self.row(part, group), self.s_recv.at[part, step])

    def settle(self):
        core = self.p.core
        for j in range(3):
            self.first_copy(j).wait_send()

        @pl.when(core == 0)
        def _():
            for j in range(3):
                self.own_copy(j).wait_send()

        def settle_step(step, carry):
            for part in range(2):
                @pl.when(step < self.last)
                def _():
                    self.z_copy(part, step).wait_send()

                @pl.when((step <= self.last) & (step > 0))
                def _():
                    self.sib_copy(part, step).wait_send()

            @pl.when((step <= self.last) & (step >= core))
            def _():
                for way in range(2):
                    self.y_copy(way, step).wait_send()
                    self.half_copy(way, step).wait_send()

            return carry

        lax.fori_loop(0, STEPS, settle_step, 0)


def columns_of(x):
    return (x % 2) * 2 + x // 2


def layer_kernel(
    q_ref, kv_ref, piece_ref, out_ref, buf, w, pieces, heads, top, acc,
    wx_send, wx_recv, ax_send, ax_recv, ah_send, ah_recv, *sems,
):
    p = Place()
    keys_values = Spread(
        p, lambda part, z, y: buf.at[part, z, y], lambda part, z: buf.at[part, z],
        lambda block, way: block.at[pl.ds(way * 64, 64)], sems[:14],
    )
    groups = (pl.ds(0, 3), pl.ds(3, 1))
    halves = (pl.ds(0, 2), pl.ds(2, 1))
    weights = Spread(
        p, lambda part, z, y: w.at[z, y, groups[part]], lambda part, z: w.at[z, :, groups[part]],
        lambda block, way: block.at[halves[way]], sems[14:],
    )
    barrier = p.greet(p.ring_neighbours() + [dict(x=(p.x + j) % 4) for j in (1, 2, 3)])
    top[...] = jnp.full_like(top, -1e30)
    acc[...] = jnp.zeros_like(acc)
    buf[p.core, p.z, p.y] = kv_ref[...]
    pieces[p.x] = piece_ref[columns_of(p.x)]
    pl.semaphore_wait(barrier, 9)

    def kv_swap():
        ref = buf.at[p.core, p.z, p.y]
        return p.copy(ref, ref, keys_values.w_send.at[0], keys_values.w_recv.at[0], core=1 - p.core)

    def w_swap(xl):
        ref = w.at[p.z, p.y, 2 * xl + p.core]
        return p.copy(ref, ref, weights.w_send.at[xl], weights.w_recv.at[xl], core=1 - p.core)

    def piece_copy(j):
        x = (p.x + j) % 4
        return p.copy(piece_ref.at[columns_of(x)], pieces.at[p.x], wx_send.at[j - 1],
                      wx_recv.at[j - 1], x=x)

    def piece_from(j):
        x = (p.x + 4 - j) % 4
        return p.copy(pieces.at[x], pieces.at[x], wx_send.at[j - 1], wx_recv.at[j - 1], x=x)

    kv_swap().start()
    for j in (1, 2, 3):
        piece_copy(j).start()
    keys_values.waits(buf.at[1 - p.core, p.z, p.y], keys_values.w_recv.at[0])
    keys_values.begin()
    for j in (1, 2, 3):
        piece_from(j).wait_recv()
    for xl in range(2):
        w[p.z, p.y, 2 * xl + p.core] = pieces[xl] + pieces[2 + xl]
        w_swap(xl).start()
    keys_values.begin_b()
    for xl in range(2):
        weights.waits(w.at[p.z, p.y, 2 * xl + 1 - p.core], weights.w_recv.at[xl])
    weights.begin()

    def attend(group, masked):
        block = jnp.concatenate(
            [buf[0, group].reshape(NY * BLK, 2 * HD), buf[1, group].reshape(NY * BLK, 2 * HD)], axis=0
        )
        keys = block[:, :HD]
        values = block[:, HD:]
        values = jnp.concatenate([values, jnp.ones_like(values)], axis=1)
        if masked:
            lane = lax.broadcasted_iota(jnp.int32, (BLK, 2 * NY * BLK), 1)
            position = (((lane // BLK) % NY) * 2 + lane // (NY * BLK)) * BLK + lane % BLK
            row = lax.broadcasted_iota(jnp.int32, (BLK, 2 * NY * BLK), 0)
            allowed = position <= (p.y * 2 + p.core) * BLK + row
        for head in range(HEADS):
            rows = pl.ds(head * BLK, BLK)
            scores = lax.dot_general(
                q_ref[:, head * HD:(head + 1) * HD], keys, NT, preferred_element_type=F32
            ) * SCORE_SCALE
            if masked:
                scores = jnp.where(allowed, scores, F32(-1e30))
            old = top[rows, :]
            new = jnp.maximum(old, jnp.max(scores, axis=1, keepdims=True))
            top[rows, :] = new
            shrink = jnp.exp2(old - new)
            expo = jnp.exp2(scores - new[:, :1]).astype(BF)
            added = jnp.dot(expo, values, preferred_element_type=F32)
            acc[rows, :] = acc[rows, :] * jnp.concatenate([shrink, shrink], axis=1) + added

    def turn(step, carry):
        keys_values.along_z(step)
        keys_values.along_y(step)

        @pl.when(step == 1)
        def _():
            weights.begin_b()

        weights.along_z(step)
        weights.along_y(step)

        @pl.when(step == 3)
        def _():
            keys_values.own_arrived()
            attend(p.z, True)
            weights.own_arrived()

        def part(j, carry):
            way = (p.core + j) % 2
            back = step - 2 - j
            here = (back >= 1) & (back <= 8 - way)
            group = keys_values.group(way, back)

            @pl.when(here & (j == 1))
            def _():
                keys_values.sib_arrived(back)
                weights.sib_arrived(back)

            @pl.when(here & (group < p.z))
            def _():
                attend(group, False)

            return carry

        lax.fori_loop(0, 2, part, 0)
        return carry

    lax.fori_loop(1, TURNS, turn, 0)

    depth = NZ * NY * PIECE
    row = lax.broadcasted_iota(jnp.int32, (QCOLS, depth), 0)
    lane = lax.broadcasted_iota(jnp.int32, (QCOLS, depth), 1)
    spot = (lane // PIECE) * (PIECE - 2) + lane % PIECE
    widen = ((row == spot) & (lane % PIECE < PIECE - 2)).astype(F32).astype(BF)
    attended = jnp.concatenate(
        [(acc[pl.ds(head * BLK, BLK), :HD] / acc[pl.ds(head * BLK, BLK), HD:]).astype(BF)
         for head in range(HEADS)], axis=1
    )
    heads[p.x] = jnp.dot(attended, widen, preferred_element_type=F32).astype(BF)

    def heads_copy(way):
        ref = heads.at[p.x]
        return p.copy(ref, ref, ax_send.at[way], ax_recv.at[way], x=(p.x + 1 + 2 * way) % 4)

    def heads_half(way):
        ref = heads.at[(p.x + 3 + 2 * way) % 4, pl.ds(way * 64, 64)]
        return p.copy(ref, ref, ah_send.at[way], ah_recv.at[way], x=(p.x + 1 + 2 * way) % 4)

    def product(x):
        rows = w[:, :, columns_of(x)].reshape(depth, QCOLS)
        return jnp.dot(heads[x], rows, preferred_element_type=F32)

    heads_copy(0).start()
    heads_copy(1).start()
    total = product(p.x)
    for way in range(2):
        heads_copy(way).wait_recv()
        heads_half(way).start()
    total += product((p.x + 3) % 4)
    total += product((p.x + 1) % 4)
    for way in range(2):
        heads_half(way).wait_recv()
    total += product((p.x + 2) % 4)
    out_ref[...] = total.astype(BF)

    kv_swap().wait_send()
    for xl in range(2):
        w_swap(xl).wait_send()
    for j in (1, 2, 3):
        piece_copy(j).wait_send()
    for way in range(2):
        heads_copy(way).wait_send()
        heads_half(way).wait_send()
    keys_values.settle()
    weights.settle()


def layer(queries, keys_values, w_out):
    xh = lax.axis_index("ctx") % 2
    rows = w_out.shape[0]
    piece = jnp.where(
        xh == 0,
        jnp.pad(w_out, ((0, PIECE - rows), (0, 0))),
        jnp.pad(w_out, ((rows, PIECE - 2 * rows), (0, 0))),
    )
    piece = jnp.transpose(piece.reshape(PIECE, 4, QCOLS), (1, 0, 2))
    return pl.pallas_call(
        layer_kernel,
        out_shape=jax.ShapeDtypeStruct((BLK, QCOLS), BF),
        in_specs=[VMEM, VMEM, VMEM],
        out_specs=VMEM,
        scratch_shapes=[
            pltpu.VMEM((2, NZ, NY, BLK, 2 * HD), BF),
            pltpu.VMEM((NZ, NY, 4, PIECE, QCOLS), BF),
            pltpu.VMEM((4, PIECE, QCOLS), BF),
            pltpu.VMEM((4, BLK, NZ * NY * PIECE), BF),
            pltpu.VMEM((HEADS * BLK, HD), F32),
            pltpu.VMEM((HEADS * BLK, 2 * HD), F32),
            DMA((3,)), DMA((3,)), DMA((2,)), DMA((2,)), DMA((2,)), DMA((2,)),
            *SPREAD_SEMS, *SPREAD_SEMS,
        ],
        compiler_params=pltpu.CompilerParams(
            collective_id=0, has_side_effects=True, vmem_limit_bytes=50 * 2**20
        ),
        name="layer",
    )(queries, keys_values, piece)


def swap_core(value):
    pairs = []
    for ctx in range(lax.axis_size("ctx")):
        for tp in range(lax.axis_size("tp")):
            xh, core = ctx % 2, tp % 2
            pairs.append((ctx * 4 + tp, (ctx - xh + core) * 4 + tp - core + xh))
    return lax.ppermute(value, ("ctx", "tp"), pairs)


def body(q_text, kv_text, patch_rows, image_count, w_out):
    tok = q_text.shape[0]
    qcols = q_text.shape[1]
    width = patch_rows.shape[1]
    img_rows = patch_rows.shape[0]
    shards = lax.axis_size("ctx")
    me = lax.axis_index("ctx")
    cap = (tok + shards - 1) // shards
    ends = jnp.cumsum(image_count)
    starts = ends - image_count
    row_ids = jnp.arange(img_rows, dtype=jnp.int32)
    image_index = me + shards * row_ids
    target = jnp.sum((ends[None, :] <= image_index[:, None]).astype(jnp.int32), axis=1)
    below = jnp.sum((target[None, :] < target[:, None]).astype(jnp.int32), axis=1)
    slot_of = target * cap + row_ids - below
    placing = (jnp.arange(shards * cap, dtype=jnp.int32)[:, None] == slot_of[None, :]).astype(BF)
    outgoing = jnp.dot(placing, patch_rows, preferred_element_type=F32).astype(BF)
    incoming = lax.all_to_all(
        outgoing.reshape(shards, cap, width), "ctx", split_axis=0, concat_axis=0, tiled=True
    )
    my_count = jnp.take(image_count, me)
    my_start = jnp.take(starts, me)
    local = jnp.arange(tok, dtype=jnp.int32)
    first = tok - my_count
    is_image = local >= first
    index = jnp.clip(my_start + local - first, 0, shards * img_rows - 1)
    source = index % shards
    lowest = (my_start - source + shards - 1) // shards
    pick = source * cap + jnp.clip(index // shards - lowest, 0, cap - 1)
    picked = jnp.take(incoming.reshape(shards * cap, width), pick, axis=0)
    text = jnp.concatenate([q_text, kv_text], axis=1)
    rows = jnp.where(is_image[:, None], picked, text)
    rows = swap_core(rows)
    return swap_core(layer(rows[:, :qcols], rows[:, qcols:], w_out))


def solution(mesh):
    in_specs = (P("ctx", "tp"), P("ctx", "tp"), P("ctx", "tp"), P(), P(("tp", "ctx"), None))
    out_specs = P("ctx", "tp")
    return jax.shard_map(body, mesh=mesh, in_specs=in_specs, out_specs=out_specs, check_vma=False)
```

time: 598 us -> 156 us (0.26)
  waiting for transfers between devices: 377 us -> 26.7 us
  Pallas kernels: 0 us -> 85.2 us
  matrix products: 61.1 us -> 0.22 us
  starting transfers between devices: 83.8 us -> 34.3 us
  other arithmetic: 34.3 us -> 1.72 us
  local copies, waits for them, and re-layouts: 24.2 us -> 5.81 us
  between operations: 15.9 us -> 1.44 us
    all_gather x2 -> x0, waiting for transfers between devices: 279 us -> none  [the longest x1 182 us: body(): piece = lax.all_gather(key_value, 'ctx', axis=0, tiled=True)]
    pallas_call x0 -> x1, Pallas kernels: none -> 85.2 us  [layer(): pl.pallas_call(layer_kernel, out_shape=jax.ShapeDtypeStruct((BLK, QCOLS),...]
    dot_general x6 -> x1, matrix products: 61.1 us -> 0.22 us  [body(): jnp.dot(placing, patch_rows, preferred_element_type=F32).astype(BF)]
    ppermute x14 -> x2, starting transfers between devices: 60.7 us -> 11.4 us  [swap_core(): return lax.ppermute(value, ('ctx', 'tp'), pairs)]
    ppermute x14 -> x2, waiting for transfers between devices: 50.7 us -> 9.47 us  [swap_core(): return lax.ppermute(value, ('ctx', 'tp'), pairs)]
    unnamed x4 -> x0, waiting for transfers between devices: 31.5 us -> none
    reduce_sum x2 -> x0, other arithmetic: 28.9 us -> none  [half_step(): total = jnp.sum(expo, axis=-1)]
    unnamed x11 -> x14, local copies, waits for them, and re-layouts: 13.5 us -> 3 us
  transfers between devices with their start and end apart: 18 -> 3, of which waited for: 16 -> 3; matrix products, arithmetic and copies ran while one was open for 18% -> 1% of each run, Pallas kernels for 0% -> 0%
where the time goes in v3:
time: 156 us; the launch traced here: 155 us
  Pallas kernels  85.2 us (55%)
  starting transfers between devices  34.3 us (22%)
  waiting for transfers between devices  26.7 us (17%)
  local copies, waits for them, and re-layouts  5.81 us (4%)
  other arithmetic  1.72 us (1%)
    pallas_call x1, Pallas kernels, layer(): pl.pallas_call(layer_kernel, out_shape=jax.ShapeDtypeStruct((BLK, QCOLS),...  85.2 us
    all_to_all x1, starting transfers between devices, body(): lax.all_to_all(outgoing.reshape(shards, cap, width), 'ctx', split_axis=0,...  23 us
    all_to_all x1, waiting for transfers between devices, body(): lax.all_to_all(outgoing.reshape(shards, cap, width), 'ctx', split_axis=0,...  17.3 us
    ppermute x2, starting transfers between devices, swap_core(): return lax.ppermute(value, ('ctx', 'tp'), pairs)  11.4 us
    ppermute x2, waiting for transfers between devices, swap_core(): return lax.ppermute(value, ('ctx', 'tp'), pairs)  9.47 us
  transfers between devices with their start and end apart: 3, of which 3 were waited for; matrix products, arithmetic and copies ran while one was open for 1% of the time, Pallas kernels for 0%

profile of v3, /device:TPU:1, one launch (start us, length us, event | category | flops | bytes accessed | tf_op | source)
XLA Modules:
  0.0 155.4 jit_solution(11127354757359943264)
XLA Ops:
  0.0 0.0 copy-start
  0.0 0.0 copy-start.4
  0.0 0.7 copy-done.4
  0.7 0.1 copy.15
  0.8 0.2 reduce-window.8
  1.0 0.1 reduce
  1.1 0.2 convert_reduce_fusion.1
  1.3 0.2 convert_reduce_fusion
  1.5 0.0 copy-done
  1.5 0.2 fusion
  1.7 0.5 broadcast.314
  2.2 0.8 reduce.1
  3.0 1.0 reshape.275
  4.0 23.0 %all-to-all-start = ((bf16[128,2,576]{2,1,0:T(2,128)(2,1)}), bf16[128,2,576]{2,1,0:T(2,128)(2,1)S(1)}, u32[]{:S(2)}, u32[]{:S(2)}) async-start(bf16[128,2,576]{2,1,0:T(2,128)(2,1)} %reshape.275), calls=%async_computation | async-start | bytes 655360 | tf_op jit(solution)/shard_map/all_to_all | solution.py:447
  27.0 0.7 dynamic-slice.4
  27.7 0.6 dynamic-slice.5
  29.6 17.3 %all-to-all-done = bf16[128,2,576]{2,1,0:T(2,128)(2,1)S(1)} async-done(((bf16[128,2,576]{2,1,0:T(2,128)(2,1)}), bf16[128,2,576]{2,1,0:T(2,128)(2,1)S(1)}, u32[]{:S(2)}, u32[]{:S(2)}) %all-to-all-start) | async-done | bytes 294944 | tf_op jit(solution)/shard_map/all_to_all | solution.py:447
  46.9 0.5 reshape.276
  47.4 0.0 copy-start.1
  47.5 0.0 copy-start.2
  47.5 0.9 gather_fusion
  48.4 0.0 copy-done.1
  48.4 0.0 copy-done.2
  48.4 0.0 copy-start.3
  48.4 0.2 maximum_select_fusion
  48.6 7.7 %collective-permute-start = (bf16[128,1152]{1,0:T(8,128)(2,1)S(1)}, bf16[128,1152]{1,0:T(8,128)(2,1)S(1)}, u32[]{:S(2)}, u32[]{:S(2)}) collective-permute-start(bf16[128,1152]{1,0:T(8,128)(2,1)S(1)} %maximum_select_fusion), channel_id=1, source_target_pairs={{0,0},{1,4},{2,2},{3,6},{4,1},{5,5},{6,3},{7,7},{8,8},{9,12},{10,1... | collective-permute-start | bytes 884744 | tf_op jit(solution)/shard_map/ppermute | solution.py:427
  56.3 0.0 copy-done.3
  56.4 4.3 %collective-permute-done = bf16[128,1152]{1,0:T(8,128)(2,1)S(1)} collective-permute-done((bf16[128,1152]{1,0:T(8,128)(2,1)S(1)}, bf16[128,1152]{1,0:T(8,128)(2,1)S(1)}, u32[]{:S(2)}, u32[]{:S(2)}) %collective-permute-start) | collective-permute-done | bytes 294944 | tf_op jit(solution)/shard_map/ppermute | solution.py:427
  60.7 85.2 %layer.1 = bf16[128,896]{1,0:T(8,128)(2,1)S(1)} custom-call(bf16[128,896]{1,0:T(8,128)(2,1)S(1)} %slice.20.q_ref, bf16[128,256]{1,0:T(8,128)(2,1)S(1)} %slice.21.kv_ref, bf16[4,16,896]{2,1,0:T(8,128)(2,1)S(1)} %bitcast.19), custom_call_target="tpu_custom_call" | custom-call | tf_op jit(solution)/shard_map/layer/pallas_call | solution.py:399
  145.9 3.7 %collective-permute-start.1 = (bf16[128,896]{1,0:T(8,128)(2,1)S(1)}, bf16[128,896]{1,0:T(8,128)(2,1)S(1)}, u32[]{:S(2)}, u32[]{:S(2)}) collective-permute-start(bf16[128,896]{1,0:T(8,128)(2,1)S(1)} %layer.1), channel_id=1, source_target_pairs={{0,0},{1,4},{2,2},{3,6},{4,1},{5,5},{6,3},{7,7},{8,8},{9,12},{10,1... | collective-permute-start | bytes 688136 | tf_op jit(solution)/shard_map/ppermute | solution.py:427
  149.6 5.2 %collective-permute-done.1 = bf16[128,896]{1,0:T(8,128)(2,1)S(1)} collective-permute-done((bf16[128,896]{1,0:T(8,128)(2,1)S(1)}, bf16[128,896]{1,0:T(8,128)(2,1)S(1)}, u32[]{:S(2)}, u32[]{:S(2)}) %collective-permute-start.1) | collective-permute-done | bytes 229408 | tf_op jit(solution)/shard_map/ppermute | solution.py:427
  154.8 0.7 copy.26
  (11 shorter events, 0.2 us)
Async XLA Ops:
  0.0 1.5 copy-start
  0.0 0.7 copy-start.4
  4.0 42.8 %all-to-all-start = ((bf16[128,2,576]{2,1,0:T(2,128)(2,1)}), bf16[128,2,576]{2,1,0:T(2,128)(2,1)S(1)}, u32[]{:S(2)}, u32[]{:S(2)}) async-start(bf16[128,2,576]{2,1,0:T(2,128)(2,1)} %reshape.275), calls=%async_computation | async-start | bytes 655360 | tf_op jit(solution)/shard_map/all_to_all | solution.py:447
  47.4 0.9 copy-start.1
  47.5 0.9 copy-start.2
  48.4 7.9 %copy-start.3 = (bf16[7,3584]{1,0:T(8,128)(2,1)S(1)}, bf16[7,3584]{1,0:T(8,128)(2,1)}, u32[]{:S(2)}) copy-start(bf16[7,3584]{1,0:T(8,128)(2,1)} %param.9) | copy-start | bytes 150532
  48.6 12.1 %collective-permute-start = (bf16[128,1152]{1,0:T(8,128)(2,1)S(1)}, bf16[128,1152]{1,0:T(8,128)(2,1)S(1)}, u32[]{:S(2)}, u32[]{:S(2)}) collective-permute-start(bf16[128,1152]{1,0:T(8,128)(2,1)S(1)} %maximum_select_fusion), channel_id=1, source_target_pairs={{0,0},{1,4},{2,2},{3,6},{4,1},{5,5},{6,3},{7,7},{8,8},{9,12},{10,1... | collective-permute-start | bytes 884744 | tf_op jit(solution)/shard_map/ppermute | solution.py:427
  145.9 8.8 %collective-permute-start.1 = (bf16[128,896]{1,0:T(8,128)(2,1)S(1)}, bf16[128,896]{1,0:T(8,128)(2,1)S(1)}, u32[]{:S(2)}, u32[]{:S(2)}) collective-permute-start(bf16[128,896]{1,0:T(8,128)(2,1)S(1)} %layer.1), channel_id=1, source_target_pairs={{0,0},{1,4},{2,2},{3,6},{4,1},{5,5},{6,3},{7,7},{8,8},{9,12},{10,1... | collective-permute-start | bytes 688136 | tf_op jit(solution)/shard_map/ppermute | solution.py:427

commit v4 on v3

--- a/solution.py
+++ b/solution.py
@@ -427,40 +427,172 @@
     return lax.ppermute(value, ("ctx", "tp"), pairs)
 
 
-def body(q_text, kv_text, patch_rows, image_count, w_out):
-    tok = q_text.shape[0]
-    qcols = q_text.shape[1]
-    width = patch_rows.shape[1]
+WIDE = 640
+
+
+def route_kernel(
+    patch_ref, q_ref, kv_ref, slot_ref, source_ref, q_out, kv_out,
+    outgoing, near, onward, landed, q_in, kv_in,
+    n_send, n_recv, f_send, f_recv, t_send, t_recv,
+):
+    p = Place()
+    straight = p.xh == p.core
+    j_me = p.y * 2 + p.xh
+
+    def near_device(i):
+        return dict(y=i // 2, x=p.core * 2 + p.xl, core=i % 2)
+
+    def near_source(j):
+        return dict(y=j // 2, x=(j % 2) * 2 + p.xl, core=p.xh)
+
+    def is_me(i):
+        return straight & (p.y * 2 + p.core == i)
+
+    barrier = pltpu.get_barrier_semaphore()
+    for j in range(8):
+        @pl.when(jnp.logical_not(is_me(j)))
+        def _():
+            pl.semaphore_signal(barrier, inc=1, device_id=p.device(**near_source(j)),
+                                device_id_type=MESH)
+    for i in range(1, NZ):
+        pl.semaphore_signal(barrier, inc=1, device_id=p.device(z=(p.z + i) % NZ),
+                            device_id_type=MESH)
+
+    lane = lax.broadcasted_iota(jnp.int32, (BLK, patch_ref.shape[0]), 0)
+    placing = (lane == slot_ref[...]).astype(F32).astype(BF)
+    outgoing[...] = jnp.dot(placing, patch_ref[...], preferred_element_type=F32).astype(BF)
+
+    @pl.when(straight)
+    def _():
+        pl.semaphore_wait(barrier, 22)
+
+    @pl.when(jnp.logical_not(straight))
+    def _():
+        pl.semaphore_wait(barrier, 23)
+
+    def near_copy(i):
+        return p.copy(outgoing.at[pl.ds(i * NZ, NZ)], near.at[j_me], n_send.at[i], n_recv.at[j_me],
+                      **near_device(i))
+
+    def near_arrival(j):
+        return p.copy(near.at[j], near.at[j], n_send.at[j], n_recv.at[j], **near_source(j))
+
+    def far_copy(i):
+        z = (p.z + i) % NZ
+        return p.copy(onward.at[z], landed.at[p.z], f_send.at[i], f_recv.at[p.z], z=z)
+
+    def far_arrival(i):
+        z = (p.z + i) % NZ
+        return p.copy(landed.at[z], landed.at[z], f_send.at[i], f_recv.at[z], z=z)
+
+    def text_copies():
+        to = dict(x=p.core * 2 + p.xl, core=p.xh)
+        return (p.copy(q_ref, q_in, t_send.at[0], t_recv.at[0], **to),
+                p.copy(kv_ref, kv_in, t_send.at[1], t_recv.at[1], **to))
+
+    for i in range(8):
+        @pl.when(jnp.logical_not(is_me(i)))
+        def _():
+            near_copy(i).start()
+
+        @pl.when(is_me(i))
+        def _():
+            near[i] = outgoing[i * NZ:(i + 1) * NZ, :]
+
+    @pl.when(jnp.logical_not(straight))
+    def _():
+        for copy in text_copies():
+            copy.start()
+
+    @pl.when(straight)
+    def _():
+        q_in[...] = q_ref[...]
+        kv_in[...] = kv_ref[...]
+
+    for j in range(8):
+        @pl.when(jnp.logical_not(is_me(j)))
+        def _():
+            near_arrival(j).wait_recv()
+
+    held = near[...].reshape(8 * NZ, HEADS * HD + 2 * HD)
+    row = lax.broadcasted_iota(jnp.int32, (NZ * 16, 8 * NZ), 0)
+    lane = lax.broadcasted_iota(jnp.int32, (NZ * 16, 8 * NZ), 1)
+    wanted = (row % 16) // 2 * NZ + row // 16
+    second = row % 2 == 1
+    zeros = jnp.zeros((8 * NZ, 2 * WIDE - held.shape[1]), BF)
+    onward[...] = (
+        jnp.dot(((lane == wanted) & jnp.logical_not(second)).astype(F32).astype(BF),
+                held[:, :WIDE], preferred_element_type=F32)
+        + jnp.dot(((lane == wanted) & second).astype(F32).astype(BF),
+                  jnp.concatenate([held[:, WIDE:], zeros], axis=1), preferred_element_type=F32)
+    ).astype(BF).reshape(NZ, 16, WIDE)
+    order = (8, 7, 9, 6, 10, 5, 11, 4, 12, 3, 13, 2, 14, 1, 15)
+    for i in order:
+        far_copy(i).start()
+    landed[p.z] = onward[p.z]
+
+    @pl.when(jnp.logical_not(straight))
+    def _():
+        for copy in text_copies():
+            copy.wait()
+
+    for i in order:
+        far_arrival(i).wait_recv()
+
+    rows = landed[...].reshape(NZ * 16, WIDE)
+    source = source_ref[...]
+    lane = lax.broadcasted_iota(jnp.int32, (BLK, NZ * 16), 1)
+    first = jnp.dot((lane == source * 2).astype(F32).astype(BF), rows, preferred_element_type=F32)
+    rest = jnp.dot((lane == source * 2 + 1).astype(F32).astype(BF), rows, preferred_element_type=F32)
+    picked = jnp.concatenate([first, rest[:, :q_ref.shape[1] + kv_ref.shape[1] - WIDE]], axis=1)
+    is_image = source >= 0
+    cut = q_ref.shape[1]
+    q_out[...] = jnp.where(is_image, picked[:, :cut], q_in[...].astype(F32)).astype(BF)
+    kv_out[...] = jnp.where(is_image, picked[:, cut:], kv_in[...].astype(F32)).astype(BF)
+
+    for i in range(8):
+        @pl.when(jnp.logical_not(is_me(i)))
+        def _():
+            near_copy(i).wait_send()
+    for i in order:
+        far_copy(i).wait_send()
+
+
+def route(patch_rows, q_text, kv_text, image_count):
     img_rows = patch_rows.shape[0]
     shards = lax.axis_size("ctx")
     me = lax.axis_index("ctx")
-    cap = (tok + shards - 1) // shards
     ends = jnp.cumsum(image_count)
-    starts = ends - image_count
-    row_ids = jnp.arange(img_rows, dtype=jnp.int32)
-    image_index = me + shards * row_ids
+    image_index = me + shards * jnp.arange(img_rows, dtype=jnp.int32)
     target = jnp.sum((ends[None, :] <= image_index[:, None]).astype(jnp.int32), axis=1)
-    below = jnp.sum((target[None, :] < target[:, None]).astype(jnp.int32), axis=1)
-    slot_of = target * cap + row_ids - below
-    placing = (jnp.arange(shards * cap, dtype=jnp.int32)[:, None] == slot_of[None, :]).astype(BF)
-    outgoing = jnp.dot(placing, patch_rows, preferred_element_type=F32).astype(BF)
-    incoming = lax.all_to_all(
-        outgoing.reshape(shards, cap, width), "ctx", split_axis=0, concat_axis=0, tiled=True
-    )
-    my_count = jnp.take(image_count, me)
-    my_start = jnp.take(starts, me)
-    local = jnp.arange(tok, dtype=jnp.int32)
-    first = tok - my_count
-    is_image = local >= first
-    index = jnp.clip(my_start + local - first, 0, shards * img_rows - 1)
-    source = index % shards
-    lowest = (my_start - source + shards - 1) // shards
-    pick = source * cap + jnp.clip(index // shards - lowest, 0, cap - 1)
-    picked = jnp.take(incoming.reshape(shards * cap, width), pick, axis=0)
-    text = jnp.concatenate([q_text, kv_text], axis=1)
-    rows = jnp.where(is_image[:, None], picked, text)
-    rows = swap_core(rows)
-    return swap_core(layer(rows[:, :qcols], rows[:, qcols:], w_out))
+    slot = (target % 8) * NZ + target // 8
+    mine = me - me % 2 + lax.axis_index("tp") % 2
+    first = BLK - jnp.take(image_count, mine)
+    local = jnp.arange(BLK, dtype=jnp.int32)
+    index = jnp.take(ends, mine) - BLK + local
+    source = jnp.where(local >= first, index % shards, -1)
+    return pl.pallas_call(
+        route_kernel,
+        out_shape=[jax.ShapeDtypeStruct(q_text.shape, BF), jax.ShapeDtypeStruct(kv_text.shape, BF)],
+        in_specs=[VMEM] * 5,
+        out_specs=[VMEM] * 2,
+        scratch_shapes=[
+            pltpu.VMEM((BLK, patch_rows.shape[1]), BF),
+            pltpu.VMEM((8, NZ, patch_rows.shape[1]), BF),
+            pltpu.VMEM((NZ, 16, WIDE), BF), pltpu.VMEM((NZ, 16, WIDE), BF),
+            pltpu.VMEM(q_text.shape, BF), pltpu.VMEM(kv_text.shape, BF),
+            DMA((8,)), DMA((8,)), DMA((NZ,)), DMA((NZ,)), DMA((2,)), DMA((2,)),
+        ],
+        compiler_params=pltpu.CompilerParams(
+            collective_id=1, has_side_effects=True, vmem_limit_bytes=24 * 2**20
+        ),
+        name="route",
+    )(patch_rows, q_text, kv_text, slot[None, :], source[:, None])
+
+
+def body(q_text, kv_text, patch_rows, image_count, w_out):
+    queries, keys_values = route(patch_rows, q_text, kv_text, image_count)
+    return swap_core(layer(queries, keys_values, w_out))
 
 
 def solution(mesh):

time: 156 us -> 139 us (0.89)
  Pallas kernels: 85.2 us -> 124 us
  starting transfers between devices: 34.3 us -> 4.57 us
  waiting for transfers between devices: 26.7 us -> 4.26 us
  local copies, waits for them, and re-layouts: 5.81 us -> 3.54 us
    pallas_call x0 -> x1, Pallas kernels: none -> 41.1 us  [route(): pl.pallas_call(route_kernel, out_shape=[jax.ShapeDtypeStruct(q_text.shape...]
    all_to_all x1 -> x0, starting transfers between devices: 23 us -> none  [body(): lax.all_to_all(outgoing.reshape(shards, cap, width), 'ctx', split_axis=0,...]
    all_to_all x1 -> x0, waiting for transfers between devices: 17.3 us -> none  [body(): lax.all_to_all(outgoing.reshape(shards, cap, width), 'ctx', split_axis=0,...]
    ppermute x2 -> x1, starting transfers between devices: 11.4 us -> 4.57 us  [swap_core(): return lax.ppermute(value, ('ctx', 'tp'), pairs)]
    ppermute x2 -> x1, waiting for transfers between devices: 9.47 us -> 4.26 us  [swap_core(): return lax.ppermute(value, ('ctx', 'tp'), pairs)]
    pallas_call x1, Pallas kernels: 85.2 us -> 83 us  [layer(): pl.pallas_call(layer_kernel, out_shape=jax.ShapeDtypeStruct((BLK, QCOLS),...]
  transfers between devices with their start and end apart: 3 -> 1, of which waited for: 3 -> 1; matrix products, arithmetic and copies ran while one was open for 1% -> 0% of each run, Pallas kernels for 0% -> 0%
where the time goes in v4:
time: 139 us; the launch traced here: 138 us
  Pallas kernels  124 us (89%)
  starting transfers between devices  4.57 us (3%)
  waiting for transfers between devices  4.26 us (3%)
  local copies, waits for them, and re-layouts  3.54 us (3%)
    pallas_call x1, Pallas kernels, layer(): pl.pallas_call(layer_kernel, out_shape=jax.ShapeDtypeStruct((BLK, QCOLS),...  83 us
    pallas_call x1, Pallas kernels, route(): pl.pallas_call(route_kernel, out_shape=[jax.ShapeDtypeStruct(q_text.shape...  41.1 us
    ppermute x1, starting transfers between devices, swap_core(): return lax.ppermute(value, ('ctx', 'tp'), pairs)  4.57 us
    ppermute x1, waiting for transfers between devices, swap_core(): return lax.ppermute(value, ('ctx', 'tp'), pairs)  4.26 us
  transfers between devices with their start and end apart: 1, of which 1 were waited for; matrix products, arithmetic and copies ran while one was open for 0% of the time, Pallas kernels for 0%

profile of v4, /device:TPU:1, one launch (start us, length us, event | category | flops | bytes accessed | tf_op | source)
XLA Modules:
  0.0 138.4 jit_solution(5224598168493935209)
XLA Ops:
  0.0 0.0 copy-start.4
  0.0 0.6 copy-done.4
  0.7 0.6 dynamic-slice.4
  1.2 0.1 copy.9
  1.3 0.2 reduce-window.8
  1.5 0.0 copy-start.3
  1.5 0.6 constant_dynamic-slice_fusion
  2.1 0.1 reduce
  3.5 0.2 convert_reduce_fusion
  3.7 0.0 copy-done.3
  3.7 0.0 copy-start
  3.8 0.0 copy-start.1
  3.8 0.0 copy-start.2
  3.9 0.8 copy-done
  4.6 0.1 copy-done.1
  4.7 0.0 copy-done.2
  4.7 41.1 %route.1 = (bf16[128,896]{1,0:T(8,128)(2,1)S(1)}, bf16[128,256]{1,0:T(8,128)(2,1)S(1)}) custom-call(bf16[64,1152]{1,0:T(8,128)(2,1)S(1)} %copy-done.1, bf16[128,896]{1,0:T(8,128)(2,1)S(1)} %copy-done, bf16[128,256]{1,0:T(8,128)(2,1)S(1)} %copy-done.2, s32[1,64]{1,0:T(1,128)S(1)} %fusion.6.slot_ref, s32[128,1]{1,0:T(8,128)S(1)} %fusion.1.source_ref), custom_call_target="tpu_custom_call" | custom-call | tf_op jit(solution)/shard_map/route/pallas_call | solution.py:574
  45.8 83.0 %layer.1 = bf16[128,896]{1,0:T(8,128)(2,1)S(1)} custom-call(bf16[128,896]{1,0:T(8,128)(2,1)S(1)} %get-tuple-element.7.q_ref, bf16[128,256]{1,0:T(8,128)(2,1)S(1)} %get-tuple-element.8.kv_ref, bf16[4,16,896]{2,1,0:T(8,128)(2,1)S(1)} %bitcast.25), custom_call_target="tpu_custom_call" | custom-call | tf_op jit(solution)/shard_map/layer/pallas_call | solution.py:399
  128.9 4.6 %collective-permute-start = (bf16[128,896]{1,0:T(8,128)(2,1)S(1)}, bf16[128,896]{1,0:T(8,128)(2,1)S(1)}, u32[]{:S(2)}, u32[]{:S(2)}) collective-permute-start(bf16[128,896]{1,0:T(8,128)(2,1)S(1)} %layer.1), channel_id=1, source_target_pairs={{0,0},{1,4},{2,2},{3,6},{4,1},{5,5},{6,3},{7,7},{8,8},{9,12},{10,1... | collective-permute-start | bytes 688136 | tf_op jit(solution)/shard_map/ppermute | solution.py:427
  133.4 4.3 %collective-permute-done = bf16[128,896]{1,0:T(8,128)(2,1)S(1)} collective-permute-done((bf16[128,896]{1,0:T(8,128)(2,1)S(1)}, bf16[128,896]{1,0:T(8,128)(2,1)S(1)}, u32[]{:S(2)}, u32[]{:S(2)}) %collective-permute-start) | collective-permute-done | bytes 229408 | tf_op jit(solution)/shard_map/ppermute | solution.py:427
  137.7 0.7 copy.15
  (5 shorter events, 0.1 us)
Async XLA Ops:
  0.0 0.7 copy-start.4
  1.5 2.2 %copy-start.3 = (bf16[7,3584]{1,0:T(8,128)(2,1)S(1)}, bf16[7,3584]{1,0:T(8,128)(2,1)}, u32[]{:S(2)}) copy-start(bf16[7,3584]{1,0:T(8,128)(2,1)} %param.9) | copy-start | bytes 150532
  3.7 0.9 copy-start
  3.8 1.0 copy-start.1
  3.8 1.0 copy-start.2
  128.9 8.8 %collective-permute-start = (bf16[128,896]{1,0:T(8,128)(2,1)S(1)}, bf16[128,896]{1,0:T(8,128)(2,1)S(1)}, u32[]{:S(2)}, u32[]{:S(2)}) collective-permute-start(bf16[128,896]{1,0:T(8,128)(2,1)S(1)} %layer.1), channel_id=1, source_target_pairs={{0,0},{1,4},{2,2},{3,6},{4,1},{5,5},{6,3},{7,7},{8,8},{9,12},{10,1... | collective-permute-start | bytes 688136 | tf_op jit(solution)/shard_map/ppermute | solution.py:427

commit v5 on v3

v5 whole, which is shorter than its diff:
```python
import functools

import jax
import jax.numpy as jnp
from jax import lax
from jax.experimental import pallas as pl
from jax.experimental.pallas import tpu as pltpu
from jax.sharding import PartitionSpec as P

HD = 128
HEADS = 7
BLK = 128
NZ, NY = 16, 4
BF = jnp.bfloat16
F32 = jnp.float32
NT = (((1,), (1,)), ((), ()))
SCORE_SCALE = 0.08838834764831845 * 1.4426950408889634
MESH = pl.DeviceIdType.MESH
VMEM = pl.BlockSpec(memory_space=pltpu.VMEM)
DMA = pltpu.SemaphoreType.DMA


class Place:
    def __init__(self):
        ctx = lax.axis_index("ctx")
        tp = lax.axis_index("tp")
        self.z, self.y, self.xh = ctx // 8, (ctx // 2) % 4, ctx % 2
        self.xl, self.core = tp // 2, tp % 2
        self.x = self.xh * 2 + self.xl

    def device(self, z=None, y=None, x=None, core=None):
        z = self.z if z is None else z
        y = self.y if y is None else y
        x = self.x if x is None else x
        core = self.core if core is None else core
        return ((z * 4 + y) * 2 + x // 2, (x % 2) * 2 + core)

    def copy(self, src, dst, send, recv, **where):
        return pltpu.make_async_remote_copy(
            src_ref=src, dst_ref=dst, send_sem=send, recv_sem=recv,
            device_id=self.device(**where), device_id_type=MESH,
        )

    def greet(self, **where):
        pl.semaphore_signal(pltpu.get_barrier_semaphore(), inc=1, device_id=self.device(**where),
                            device_id_type=MESH)


HOPS = 9
ROUNDS = 8
SPREAD_SEMS = [
    DMA((HOPS,)), DMA((HOPS,)), DMA((2, HOPS)), DMA((2, HOPS)), DMA((2, HOPS)), DMA((2, HOPS)),
    DMA((HOPS,)), DMA((HOPS,)), DMA((3,)), DMA((3,)),
]


class Spread:
    def __init__(self, place, everything, half, sems):
        self.p, self.all, self.half = place, everything, half
        (self.z_send, self.z_recv, self.y_send, self.y_recv, self.h_send, self.h_recv,
         self.s_send, self.s_recv, self.o_send, self.o_recv) = sems
        self.last = 8 - place.core

    def group(self, way, hop):
        return (self.p.z + NZ - hop + 2 * hop * way) % NZ

    def mine(self, hop):
        return self.all.at[self.group(self.p.core, hop), self.p.y]

    def waits(self, ref, sem):
        self.p.copy(ref, ref, self.o_send.at[0], sem, core=1 - self.p.core).wait_recv()

    def z_copy(self, hop, far):
        p, ref, end = self.p, self.mine(hop), hop + far
        return p.copy(ref, ref, self.z_send.at[end], self.z_recv.at[end],
                      z=(p.z + NZ + far - 2 * far * p.core) % NZ)

    def z_start(self, hop):
        for far in (2, 1):
            @pl.when(hop + far <= self.last)
            def _():
                self.z_copy(hop, far).start()

    def y_copy(self, way, hop):
        p, ref = self.p, self.mine(hop)
        return p.copy(ref, ref, self.y_send.at[way, hop], self.y_recv.at[way, hop],
                      y=(p.y + 1 + 2 * way) % NY)

    def half_copy(self, way, hop):
        p = self.p
        ref = self.half(self.all.at[self.group(p.core, hop), (p.y + 3 + 2 * way) % NY], way)
        return p.copy(ref, ref, self.h_send.at[way, hop], self.h_recv.at[way, hop],
                      y=(p.y + 1 + 2 * way) % NY)

    def sib_copy(self, hop):
        p = self.p
        ref = self.all.at[self.group(p.core, hop)]
        return p.copy(ref, ref, self.s_send.at[hop], self.s_recv.at[hop], core=1 - p.core)

    def own_copy(self, j):
        p = self.p
        ref = self.all.at[p.z, (p.y + 1 + j) % NY]
        return p.copy(ref, ref, self.o_send.at[j], self.o_recv.at[j], core=1 - p.core)

    def begin(self):
        self.z_start(0)

        @pl.when(self.p.core == 0)
        def _():
            self.y_copy(0, 0).start()
            self.y_copy(1, 0).start()

    def there(self, hop):
        return (hop <= self.last) & (hop >= self.p.core)

    def along_z(self, hop):
        @pl.when(hop <= self.last)
        def _():
            self.waits(self.mine(hop), self.z_recv.at[hop])
            self.z_start(hop)
            self.y_copy(0, hop).start()
            self.y_copy(1, hop).start()

        @pl.when(hop - 1 <= self.last)
        def _():
            self.waits(self.mine(hop - 1), self.z_recv.at[hop - 1])
            self.y_copy(0, hop - 1).start()
            self.y_copy(1, hop - 1).start()

    def across_y(self, hop):
        @pl.when(self.there(hop))
        def _():
            for way in range(2):
                self.y_copy(way, hop).wait_recv()
                self.half_copy(way, hop).start()

    def hand_over(self, hop):
        @pl.when(self.there(hop))
        def _():
            for way in range(2):
                self.half_copy(way, hop).wait_recv()

            @pl.when(hop > 0)
            def _():
                self.sib_copy(hop).start()

            @pl.when(hop == 0)
            def _():
                for j in range(3):
                    self.own_copy(j).start()

    def own_arrived(self):
        @pl.when(self.p.core == 1)
        def _():
            for j in range(3):
                self.own_copy(j).wait_recv()

    def sib_arrived(self, hop):
        self.waits(self.all.at[self.group(1 - self.p.core, hop)], self.s_recv.at[hop])

    def settle(self):
        def settle_hop(hop, carry):
            @pl.when((hop > 0) & (hop <= self.last))
            def _():
                self.waits_sent(hop)
                self.sib_copy(hop).wait_send()

            @pl.when(self.there(hop))
            def _():
                for way in range(2):
                    self.y_copy(way, hop).wait_send()
                    self.half_copy(way, hop).wait_send()

            return carry

        lax.fori_loop(0, HOPS, settle_hop, 0)

        @pl.when(self.p.core == 0)
        def _():
            for j in range(3):
                self.own_copy(j).wait_send()

    def waits_sent(self, end):
        self.z_copy(end - 1, 1).wait_send()

    def round(self, m):
        self.along_z(2 * m)
        for hop in (2 * m - 2, 2 * m - 3):
            @pl.when(hop >= 0)
            def _():
                self.across_y(hop)
        for hop in (2 * m - 4, 2 * m - 5):
            @pl.when(hop >= 0)
            def _():
                self.hand_over(hop)


RING_SEMS = [DMA((3,)), DMA((3,)), DMA((HOPS,)), DMA((HOPS,)), DMA((HOPS,)), DMA((HOPS,))]


class Ring:
    def __init__(self, place, everything, part, sems):
        self.p, self.all, self.part = place, everything, part
        self.f_send, self.f_recv, self.z_send, self.z_recv, self.s_send, self.s_recv = sems
        self.last = 8 - place.core

    def group(self, way, step):
        return self.all.at[(self.p.z + NZ - step + 2 * step * way) % NZ, :, self.part]

    def waits(self, ref, sem):
        self.p.copy(ref, ref, self.f_send.at[0], sem, core=1 - self.p.core).wait_recv()

    def first_copy(self, j):
        p, ref = self.p, self.all.at[self.p.z, self.p.y, self.part]
        return p.copy(ref, ref, self.f_send.at[j], self.f_recv.at[j], y=(p.y + 1 + j) % NY)

    def z_copy(self, step):
        p, ref = self.p, self.group(self.p.core, step)
        return p.copy(ref, ref, self.z_send.at[step], self.z_recv.at[step + 1],
                      z=(p.z + 17 - 2 * p.core) % NZ)

    def sib_copy(self, step):
        p, ref = self.p, self.group(self.p.core, step)
        return p.copy(ref, ref, self.s_send.at[step], self.s_recv.at[step], core=1 - p.core)

    def begin(self):
        for j in range(3):
            self.first_copy(j).start()

    def set_off(self):
        for j in range(3):
            self.first_copy(j).wait_recv()
        self.z_copy(0).start()

    def step(self, step):
        @pl.when(step <= self.last)
        def _():
            self.waits(self.group(self.p.core, step), self.z_recv.at[step])

            @pl.when(step < self.last)
            def _():
                self.z_copy(step).start()

            self.sib_copy(step).start()

    def settle(self):
        for j in range(3):
            self.first_copy(j).wait_send()

        def settle_step(step, carry):
            @pl.when(step < self.last)
            def _():
                self.z_copy(step).wait_send()

            @pl.when((step > 0) & (step <= self.last))
            def _():
                self.sib_copy(step).wait_send()

            return carry

        lax.fori_loop(0, HOPS, settle_step, 0)

    def arrived(self):
        def arrival(step, carry):
            @pl.when(step <= 7 + self.p.core)
            def _():
                self.waits(self.group(1 - self.p.core, step), self.s_recv.at[step])

            return carry

        lax.fori_loop(1, HOPS, arrival, 0)


QCOLS = HEADS * HD
PIECE = 16
WIDE = 640


def columns_of(x):
    return (x % 2) * 2 + x // 2


def layer_kernel(
    patch_hbm, q_ref, kv_ref, count_hbm, w_out_hbm, out_ref,
    patch_ref, count_ref, w_out_ref, piece, outgoing, near, onward, landed, q_in, kv_in, queries,
    buf, w, pieces, heads, top, acc,
    l_sem, n_send, n_recv, f_send, f_recv, t_send, t_recv, c_send, c_recv,
    wx_send, wx_recv, ax_send, ax_recv, ah_send, ah_recv, *sems,
):
    p = Place()
    keys_values = Spread(p, buf, lambda block, way: block.at[way], sems[:10])
    rings = [Ring(p, w, pl.ds(0, 2), sems[10:16]), Ring(p, w, pl.ds(2, 2), sems[16:])]
    straight = p.xh == p.core
    j_me = p.y * 2 + p.xh
    cut = QCOLS

    def near_device(i):
        return dict(y=i // 2, x=p.core * 2 + p.xl, core=i % 2)

    def near_source(j):
        return dict(y=j // 2, x=(j % 2) * 2 + p.xl, core=p.xh)

    def is_me(i):
        return straight & (p.y * 2 + p.core == i)

    loads = [
        pltpu.make_async_copy(count_hbm, count_ref, l_sem.at[0]),
        pltpu.make_async_copy(patch_hbm, patch_ref, l_sem.at[1]),
        pltpu.make_async_copy(w_out_hbm, w_out_ref, l_sem.at[2]),
    ]
    stays = [
        pltpu.make_async_copy(q_ref, q_in, l_sem.at[3]),
        pltpu.make_async_copy(kv_ref, kv_in, l_sem.at[4]),
    ]
    for load in loads:
        load.start()

    @pl.when(straight)
    def _():
        for load in stays:
            load.start()

    for j in range(8):
        @pl.when(jnp.logical_not(is_me(j)))
        def _():
            p.greet(**near_source(j))
    for i in range(1, NZ):
        p.greet(z=(p.z + i) % NZ)
    for i in range(1, 4):
        p.greet(x=(p.x + i) % 4)
    for i in (1, 2, 3):
        p.greet(y=(p.y + i) % NY)
    p.greet(core=1 - p.core)

    for load in loads:
        load.wait()
    filled = w_out_ref.shape[0]
    row = lax.broadcasted_iota(jnp.int32, (PIECE, filled), 0)
    lane = lax.broadcasted_iota(jnp.int32, (PIECE, filled), 1)
    filling = (row == lane + filled * p.xh).astype(F32).astype(BF)
    for b in range(4):
        piece[b] = jnp.dot(filling, w_out_ref[:, b * QCOLS:(b + 1) * QCOLS],
                           preferred_element_type=F32).astype(BF)

    shards = count_ref.shape[1]
    counts = count_ref[...].astype(F32)
    row = lax.broadcasted_iota(jnp.int32, (shards, shards), 0)
    lane = lax.broadcasted_iota(jnp.int32, (shards, shards), 1)
    ends = jnp.sum(jnp.where(lane <= row, counts, F32(0.0)), axis=1, keepdims=True)
    img_rows = patch_ref.shape[0]
    image = (p.z * 4 + p.y) * 2 + p.xh + shards * lax.broadcasted_iota(
        jnp.int32, (shards, img_rows), 1)
    target = jnp.sum(
        jnp.where(ends <= image.astype(F32), F32(1.0), F32(0.0)), axis=0, keepdims=True
    ).astype(jnp.int32)
    slot = (target & 7) * NZ + (target >> 3)
    mine = (p.z * 4 + p.y) * 2 + p.core
    lane = lax.broadcasted_iota(jnp.int32, (1, shards), 1)
    my_count = jnp.sum(jnp.where(lane == mine, counts, F32(0.0)), axis=1, keepdims=True)
    my_end = jnp.sum(jnp.where(lane <= mine, counts, F32(0.0)), axis=1, keepdims=True)
    local = lax.broadcasted_iota(jnp.int32, (BLK, 1), 0)
    source = jnp.where(
        local >= BLK - my_count.astype(jnp.int32),
        (my_end.astype(jnp.int32) + local - BLK) & (shards - 1), -1
    )
    lane = lax.broadcasted_iota(jnp.int32, (BLK, img_rows), 0)
    placing = (lane == slot).astype(F32).astype(BF)
    outgoing[...] = jnp.dot(placing, patch_ref[...], preferred_element_type=F32).astype(BF)

    pieces[p.x] = piece[columns_of(p.x)]
    top[...] = jnp.full_like(top, -1e30)
    acc[...] = jnp.zeros_like(acc)

    @pl.when(straight)
    def _():
        pl.semaphore_wait(pltpu.get_barrier_semaphore(), 29)

    @pl.when(jnp.logical_not(straight))
    def _():
        pl.semaphore_wait(pltpu.get_barrier_semaphore(), 30)

    def near_copy(i):
        return p.copy(outgoing.at[pl.ds(i * NZ, NZ)], near.at[j_me], n_send.at[i], n_recv.at[j_me],
                      **near_device(i))

    def near_arrival(j):
        return p.copy(near.at[j], near.at[j], n_send.at[j], n_recv.at[j], **near_source(j))

    def far_copy(i):
        z = (p.z + i) % NZ
        return p.copy(onward.at[z], landed.at[p.z], f_send.at[i], f_recv.at[p.z], z=z)

    def far_arrival(i):
        z = (p.z + i) % NZ
        return p.copy(landed.at[z], landed.at[z], f_send.at[i], f_recv.at[z], z=z)

    def text_copies():
        to = dict(x=p.core * 2 + p.xl, core=p.xh)
        return (p.copy(q_ref, q_in, t_send.at[0], t_recv.at[0], **to),
                p.copy(kv_ref, kv_in, t_send.at[1], t_recv.at[1], **to))

    def piece_copy(j):
        x = (p.x + j) % 4
        return p.copy(piece.at[columns_of(x)], pieces.at[p.x], wx_send.at[j - 1],
                      wx_recv.at[j - 1], x=x)

    def piece_from(j):
        x = (p.x + 4 - j) % 4
        return p.copy(pieces.at[x], pieces.at[x], wx_send.at[j - 1], wx_recv.at[j - 1], x=x)

    def w_swap(xl):
        ref = w.at[p.z, p.y, 2 * xl + p.core]
        return p.copy(ref, ref, c_send.at[xl], c_recv.at[xl], core=1 - p.core)

    def kv_swap():
        ref = buf.at[p.z, p.y, p.core]
        return p.copy(ref, ref, c_send.at[2], c_recv.at[2], core=1 - p.core)

    for i in range(8):
        @pl.when(jnp.logical_not(is_me(i)))
        def _():
            near_copy(i).start()

        @pl.when(is_me(i))
        def _():
            near[i] = outgoing[i * NZ:(i + 1) * NZ, :]

    @pl.when(jnp.logical_not(straight))
    def _():
        for copy in text_copies():
            copy.start()

    for j in (1, 2, 3):
        piece_copy(j).start()

    for j in range(8):
        @pl.when(jnp.logical_not(is_me(j)))
        def _():
            near_arrival(j).wait_recv()

    held = near[...].reshape(8 * NZ, HEADS * HD + 2 * HD)
    row = lax.broadcasted_iota(jnp.int32, (NZ * 16, 8 * NZ), 0)
    lane = lax.broadcasted_iota(jnp.int32, (NZ * 16, 8 * NZ), 1)
    wanted = (row % 16) // 2 * NZ + row // 16
    second = row % 2 == 1
    zeros = jnp.zeros((8 * NZ, 2 * WIDE - held.shape[1]), BF)
    onward[...] = (
        jnp.dot(((lane == wanted) & jnp.logical_not(second)).astype(F32).astype(BF),
                held[:, :WIDE], preferred_element_type=F32)
        + jnp.dot(((lane == wanted) & second).astype(F32).astype(BF),
                  jnp.concatenate([held[:, WIDE:], zeros], axis=1), preferred_element_type=F32)
    ).astype(BF).reshape(NZ, 16, WIDE)
    order = (8, 7, 9, 6, 10, 5, 11, 4, 12, 3, 13, 2, 14, 1, 15)
    for i in order:
        far_copy(i).start()
    landed[p.z] = onward[p.z]

    for j in (1, 2, 3):
        piece_from(j).wait_recv()
    for xl in range(2):
        w[p.z, p.y, 2 * xl + p.core] = pieces[xl] + pieces[2 + xl]
        w_swap(xl).start()
    for xl in range(2):
        rings[0].waits(w.at[p.z, p.y, 2 * xl + 1 - p.core], c_recv.at[xl])
    for ring in rings:
        ring.begin()

    for ring in rings:
        ring.set_off()
    for ring in rings:
        ring.step(1)

    @pl.when(straight)
    def _():
        for load in stays:
            load.wait()

    @pl.when(jnp.logical_not(straight))
    def _():
        for copy in text_copies():
            copy.wait()

    for i in order:
        far_arrival(i).wait_recv()

    rows = landed[...].reshape(NZ * 16, WIDE)
    lane = lax.broadcasted_iota(jnp.int32, (BLK, NZ * 16), 1)
    first = jnp.dot((lane == source * 2).astype(F32).astype(BF), rows, preferred_element_type=F32)
    rest = jnp.dot((lane == source * 2 + 1).astype(F32).astype(BF), rows, preferred_element_type=F32)
    picked = jnp.concatenate([first, rest[:, :cut + 2 * HD - WIDE]], axis=1)
    is_image = source >= 0
    queries[...] = jnp.where(is_image, picked[:, :cut], q_in[...].astype(F32)).astype(BF)
    buf[p.z, p.y, p.core] = jnp.where(is_image, picked[:, cut:], kv_in[...].astype(F32)).astype(BF)
    kv_swap().start()
    keys_values.waits(buf.at[p.z, p.y, 1 - p.core], c_recv.at[2])
    keys_values.begin()

    def attend(group, masked):
        block = buf[group].reshape(2 * NY * BLK, 2 * HD)
        keys = block[:, :HD]
        values = block[:, HD:]
        values = jnp.concatenate([values, jnp.ones_like(values)], axis=1)
        if masked:
            position = lax.broadcasted_iota(jnp.int32, (BLK, 2 * NY * BLK), 1)
            row = lax.broadcasted_iota(jnp.int32, (BLK, 2 * NY * BLK), 0)
            allowed = position <= (p.y * 2 + p.core) * BLK + row
        for head in range(HEADS):
            rows = pl.ds(head * BLK, BLK)
            scores = lax.dot_general(
                queries[:, head * HD:(head + 1) * HD], keys, NT, preferred_element_type=F32
            ) * SCORE_SCALE
            if masked:
                scores = jnp.where(allowed, scores, F32(-1e30))
            old = top[rows, :]
            new = jnp.maximum(old, jnp.max(scores, axis=1, keepdims=True))
            top[rows, :] = new
            shrink = jnp.exp2(old - new)
            expo = jnp.exp2(scores - new[:, :1]).astype(BF)
            added = jnp.dot(expo, values, preferred_element_type=F32)
            acc[rows, :] = acc[rows, :] * jnp.concatenate([shrink, shrink], axis=1) + added

    def turn(m, carry):
        keys_values.round(m)
        for ring in rings:
            ring.step(m + 1)

        @pl.when(m == 3)
        def _():
            keys_values.own_arrived()
            attend(p.z, True)

        def part(j, carry):
            hop = 2 * m - 4 - j
            way = (p.core + j // 2) % 2
            group = keys_values.group(way, hop)
            here = (hop >= 1) & (hop <= 8 - way)

            @pl.when(here & (j >= 2))
            def _():
                keys_values.sib_arrived(hop)

            @pl.when(here & (group < p.z))
            def _():
                attend(group, False)

            return carry

        lax.fori_loop(0, 4, part, 0)
        return carry

    lax.fori_loop(1, ROUNDS, turn, 0)
    for ring in rings:
        ring.arrived()

    depth = NZ * NY * PIECE
    row = lax.broadcasted_iota(jnp.int32, (QCOLS, depth), 0)
    lane = lax.broadcasted_iota(jnp.int32, (QCOLS, depth), 1)
    spot = (lane // PIECE) * (PIECE - 2) + lane % PIECE
    widen = ((row == spot) & (lane % PIECE < PIECE - 2)).astype(F32).astype(BF)
    attended = jnp.concatenate(
        [(acc[pl.ds(head * BLK, BLK), :HD] / acc[pl.ds(head * BLK, BLK), HD:]).astype(BF)
         for head in range(HEADS)], axis=1
    )
    heads[p.x] = jnp.dot(attended, widen, preferred_element_type=F32).astype(BF)

    def heads_copy(way):
        ref = heads.at[p.x]
        return p.copy(ref, ref, ax_send.at[way], ax_recv.at[way], x=(p.x + 1 + 2 * way) % 4)

    def heads_half(way):
        ref = heads.at[(p.x + 3 + 2 * way) % 4, pl.ds(way * 64, 64)]
        return p.copy(ref, ref, ah_send.at[way], ah_recv.at[way], x=(p.x + 1 + 2 * way) % 4)

    def product(x):
        rows = w[:, :, columns_of(x)].reshape(depth, QCOLS)
        return jnp.dot(heads[x], rows, preferred_element_type=F32)

    heads_copy(0).start()
    heads_copy(1).start()
    total = product(p.x)
    for way in range(2):
        heads_copy(way).wait_recv()
        heads_half(way).start()
    total += product((p.x + 3) % 4)
    total += product((p.x + 1) % 4)
    for way in range(2):
        heads_half(way).wait_recv()
    total += product((p.x + 2) % 4)
    out_ref[...] = total.astype(BF)

    kv_swap().wait_send()
    for xl in range(2):
        w_swap(xl).wait_send()
    for j in (1, 2, 3):
        piece_copy(j).wait_send()
    for way in range(2):
        heads_copy(way).wait_send()
        heads_half(way).wait_send()
    keys_values.settle()
    for ring in rings:
        ring.settle()
    for i in range(8):
        @pl.when(jnp.logical_not(is_me(i)))
        def _():
            near_copy(i).wait_send()
    for i in order:
        far_copy(i).wait_send()


def layer(q_text, kv_text, patch_rows, image_count, w_out):
    width = patch_rows.shape[1]
    return pl.pallas_call(
        layer_kernel,
        out_shape=jax.ShapeDtypeStruct((BLK, QCOLS), BF),
        in_specs=[pl.BlockSpec(memory_space=pltpu.HBM)] * 5,
        out_specs=VMEM,
        scratch_shapes=[
            pltpu.VMEM(patch_rows.shape, BF), pltpu.VMEM((1, image_count.shape[0]), jnp.int32),
            pltpu.VMEM(w_out.shape, BF),
            pltpu.VMEM((4, PIECE, QCOLS), BF),
            pltpu.VMEM((BLK, width), BF),
            pltpu.VMEM((8, NZ, width), BF),
            pltpu.VMEM((NZ, 16, WIDE), BF), pltpu.VMEM((NZ, 16, WIDE), BF),
            pltpu.VMEM(q_text.shape, BF), pltpu.VMEM(kv_text.shape, BF),
            pltpu.VMEM(q_text.shape, BF),
            pltpu.VMEM((NZ, NY, 2, BLK, 2 * HD), BF),
            pltpu.VMEM((NZ, NY, 4, PIECE, QCOLS), BF),
            pltpu.VMEM((4, PIECE, QCOLS), BF),
            pltpu.VMEM((4, BLK, NZ * NY * PIECE), BF),
            pltpu.VMEM((HEADS * BLK, HD), F32),
            pltpu.VMEM((HEADS * BLK, 2 * HD), F32),
            DMA((5,)), DMA((8,)), DMA((8,)), DMA((NZ,)), DMA((NZ,)), DMA((2,)), DMA((2,)),
            DMA((3,)), DMA((3,)),
            DMA((3,)), DMA((3,)), DMA((2,)), DMA((2,)), DMA((2,)), DMA((2,)),
            *SPREAD_SEMS, *RING_SEMS, *RING_SEMS,
        ],
        compiler_params=pltpu.CompilerParams(
            collective_id=0, has_side_effects=True, vmem_limit_bytes=63 * 2**20
        ),
        name="layer",
    )(patch_rows, q_text, kv_text, image_count[None, :], w_out)


def swap_core(value):
    pairs = []
    for ctx in range(lax.axis_size("ctx")):
        for tp in range(lax.axis_size("tp")):
            xh, core = ctx % 2, tp % 2
            pairs.append((ctx * 4 + tp, (ctx - xh + core) * 4 + tp - core + xh))
    return lax.ppermute(value, ("ctx", "tp"), pairs)


def body(q_text, kv_text, patch_rows, image_count, w_out):
    return swap_core(layer(q_text, kv_text, patch_rows, image_count, w_out))


def solution(mesh):
    in_specs = (P("ctx", "tp"), P("ctx", "tp"), P("ctx", "tp"), P(), P(("tp", "ctx"), None))
    out_specs = P("ctx", "tp")
    return jax.shard_map(body, mesh=mesh, in_specs=in_specs, out_specs=out_specs, check_vma=False)
```

time: 156 us -> 132 us (0.85)
  Pallas kernels: 85.2 us -> 122 us
  starting transfers between devices: 34.3 us -> 4.63 us
  waiting for transfers between devices: 26.7 us -> 4.42 us
  local copies, waits for them, and re-layouts: 5.81 us -> 0.69 us
  other arithmetic: 1.72 us -> 0 us
    pallas_call x1, Pallas kernels: 85.2 us -> 122 us  [layer(): pl.pallas_call(layer_kernel, out_shape=jax.ShapeDtypeStruct((BLK, QCOLS),...]
    all_to_all x1 -> x0, starting transfers between devices: 23 us -> none  [body(): lax.all_to_all(outgoing.reshape(shards, cap, width), 'ctx', split_axis=0,...]
    all_to_all x1 -> x0, waiting for transfers between devices: 17.3 us -> none  [body(): lax.all_to_all(outgoing.reshape(shards, cap, width), 'ctx', split_axis=0,...]
    ppermute x2 -> x1, starting transfers between devices: 11.4 us -> 4.63 us  [swap_core(): return lax.ppermute(value, ('ctx', 'tp'), pairs)]
    ppermute x2 -> x1, waiting for transfers between devices: 9.47 us -> 4.42 us  [swap_core(): return lax.ppermute(value, ('ctx', 'tp'), pairs)]
    unnamed x14 -> x1, local copies, waits for them, and re-layouts: 3 us -> 0.69 us
  transfers between devices with their start and end apart: 3 -> 1, of which waited for: 3 -> 1; matrix products, arithmetic and copies ran while one was open for 1% -> 0% of each run, Pallas kernels for 0% -> 0%
where the time goes in v5:
time: 132 us
  Pallas kernels  122 us (92%)
  starting transfers between devices  4.63 us (4%)
  waiting for transfers between devices  4.42 us (3%)
    pallas_call x1, Pallas kernels, layer(): pl.pallas_call(layer_kernel, out_shape=jax.ShapeDtypeStruct((BLK, QCOLS),...  122 us
    ppermute x1, starting transfers between devices, swap_core(): return lax.ppermute(value, ('ctx', 'tp'), pairs)  4.63 us
    ppermute x1, waiting for transfers between devices, swap_core(): return lax.ppermute(value, ('ctx', 'tp'), pairs)  4.42 us
  transfers between devices with their start and end apart: 1, of which 1 were waited for; matrix products, arithmetic and copies ran while one was open for 0% of the time, Pallas kernels for 0%

profile of v5, /device:TPU:1, one launch (start us, length us, event | category | flops | bytes accessed | tf_op | source)
XLA Modules:
  0.0 131.8 jit_solution(7868958887176711124)
XLA Ops:
  0.0 122.1 %layer.1 = bf16[128,896]{1,0:T(8,128)(2,1)} custom-call(bf16[64,1152]{1,0:T(8,128)(2,1)} %patch_hbm.1, bf16[128,896]{1,0:T(8,128)(2,1)} %q_ref.1, bf16[128,256]{1,0:T(8,128)(2,1)} %kv_ref.1, s32[1,128]{1,0:T(1,128)} %bitcast.1, bf16[7,3584]{1,0:T(8,128)(2,1)} %w_out_hbm.1), custom_call_target="tpu_custom_call" | custom-call | tf_op jit(solution)/shard_map/layer/pallas_call | solution.py:612
  122.1 4.6 %collective-permute-start = (bf16[128,896]{1,0:T(8,128)(2,1)}, bf16[128,896]{1,0:T(8,128)(2,1)S(1)}, u32[]{:S(2)}, u32[]{:S(2)}) collective-permute-start(bf16[128,896]{1,0:T(8,128)(2,1)} %layer.1), channel_id=1, source_target_pairs={{0,0},{1,4},{2,2},{3,6},{4,1},{5,5},{6,3},{7,7},{8,8},{9,12},{10,1... | collective-permute-start | bytes 688136 | tf_op jit(solution)/shard_map/ppermute | solution.py:650
  126.7 4.4 %collective-permute-done = bf16[128,896]{1,0:T(8,128)(2,1)S(1)} collective-permute-done((bf16[128,896]{1,0:T(8,128)(2,1)}, bf16[128,896]{1,0:T(8,128)(2,1)S(1)}, u32[]{:S(2)}, u32[]{:S(2)}) %collective-permute-start) | collective-permute-done | bytes 229408 | tf_op jit(solution)/shard_map/ppermute | solution.py:650
  131.1 0.7 copy.7
Async XLA Ops:
  122.1 9.1 %collective-permute-start = (bf16[128,896]{1,0:T(8,128)(2,1)}, bf16[128,896]{1,0:T(8,128)(2,1)S(1)}, u32[]{:S(2)}, u32[]{:S(2)}) collective-permute-start(bf16[128,896]{1,0:T(8,128)(2,1)} %layer.1), channel_id=1, source_target_pairs={{0,0},{1,4},{2,2},{3,6},{4,1},{5,5},{6,3},{7,7},{8,8},{9,12},{10,1... | collective-permute-start | bytes 688136 | tf_op jit(solution)/shard_map/ppermute | solution.py:650

commit v6 on v5

--- a/solution.py
+++ b/solution.py
@@ -283,9 +283,9 @@
 def layer_kernel(
     patch_hbm, q_ref, kv_ref, count_hbm, w_out_hbm, out_ref,
     patch_ref, count_ref, w_out_ref, piece, outgoing, near, onward, landed, q_in, kv_in, queries,
-    buf, w, pieces, heads, top, acc,
+    buf, w, pieces, heads, widen, result, top, acc,
     l_sem, n_send, n_recv, f_send, f_recv, t_send, t_recv, c_send, c_recv,
-    wx_send, wx_recv, ax_send, ax_recv, ah_send, ah_recv, *sems,
+    wx_send, wx_recv, ax_send, ax_recv, ah_send, ah_recv, r_send, r_recv, *sems,
 ):
     p = Place()
     keys_values = Spread(p, buf, lambda block, way: block.at[way], sems[:10])
@@ -368,6 +368,11 @@
     outgoing[...] = jnp.dot(placing, patch_ref[...], preferred_element_type=F32).astype(BF)
 
     pieces[p.x] = piece[columns_of(p.x)]
+    depth = NZ * NY * PIECE
+    row = lax.broadcasted_iota(jnp.int32, (QCOLS, depth), 0)
+    lane = lax.broadcasted_iota(jnp.int32, (QCOLS, depth), 1)
+    spot = (lane // PIECE) * (PIECE - 2) + lane % PIECE
+    widen[...] = ((row == spot) & (lane % PIECE < PIECE - 2)).astype(F32).astype(BF)
     top[...] = jnp.full_like(top, -1e30)
     acc[...] = jnp.zeros_like(acc)
 
@@ -552,20 +557,15 @@
     for ring in rings:
         ring.arrived()
 
-    depth = NZ * NY * PIECE
-    row = lax.broadcasted_iota(jnp.int32, (QCOLS, depth), 0)
-    lane = lax.broadcasted_iota(jnp.int32, (QCOLS, depth), 1)
-    spot = (lane // PIECE) * (PIECE - 2) + lane % PIECE
-    widen = ((row == spot) & (lane % PIECE < PIECE - 2)).astype(F32).astype(BF)
     attended = jnp.concatenate(
         [(acc[pl.ds(head * BLK, BLK), :HD] / acc[pl.ds(head * BLK, BLK), HD:]).astype(BF)
          for head in range(HEADS)], axis=1
     )
-    heads[p.x] = jnp.dot(attended, widen, preferred_element_type=F32).astype(BF)
-
-    def heads_copy(way):
-        ref = heads.at[p.x]
-        return p.copy(ref, ref, ax_send.at[way], ax_recv.at[way], x=(p.x + 1 + 2 * way) % 4)
+    heads[p.x] = jnp.dot(attended, widen[...], preferred_element_type=F32).astype(BF)
+
+    def heads_copy(way, j):
+        ref = heads.at[p.x, pl.ds((way + j) % 2 * 64, 64)]
+        return p.copy(ref, ref, ax_send.at[way, j], ax_recv.at[way, j], x=(p.x + 1 + 2 * way) % 4)
 
     def heads_half(way):
         ref = heads.at[(p.x + 3 + 2 * way) % 4, pl.ds(way * 64, 64)]
@@ -575,18 +575,31 @@
         rows = w[:, :, columns_of(x)].reshape(depth, QCOLS)
         return jnp.dot(heads[x], rows, preferred_element_type=F32)
 
-    heads_copy(0).start()
-    heads_copy(1).start()
+    for j in range(2):
+        heads_copy(0, j).start()
+        heads_copy(1, j).start()
     total = product(p.x)
     for way in range(2):
-        heads_copy(way).wait_recv()
+        heads_copy(way, 0).wait_recv()
         heads_half(way).start()
+    for way in range(2):
+        heads_copy(way, 1).wait_recv()
     total += product((p.x + 3) % 4)
     total += product((p.x + 1) % 4)
     for way in range(2):
         heads_half(way).wait_recv()
     total += product((p.x + 2) % 4)
-    out_ref[...] = total.astype(BF)
+    result[...] = total.astype(BF)
+    result_copy = p.copy(result, out_ref, r_send, r_recv, x=p.core * 2 + p.xl, core=p.xh)
+
+    @pl.when(straight)
+    def _():
+        out_ref[...] = result[...]
+
+    @pl.when(jnp.logical_not(straight))
+    def _():
+        result_copy.start()
+
 
     kv_swap().wait_send()
     for xl in range(2):
@@ -594,7 +607,8 @@
     for j in (1, 2, 3):
         piece_copy(j).wait_send()
     for way in range(2):
-        heads_copy(way).wait_send()
+        heads_copy(way, 0).wait_send()
+        heads_copy(way, 1).wait_send()
         heads_half(way).wait_send()
     keys_values.settle()
     for ring in rings:
@@ -605,6 +619,10 @@
             near_copy(i).wait_send()
     for i in order:
         far_copy(i).wait_send()
+
+    @pl.when(jnp.logical_not(straight))
+    def _():
+        result_copy.wait()
 
 
 def layer(q_text, kv_text, patch_rows, image_count, w_out):
@@ -627,11 +645,13 @@
             pltpu.VMEM((NZ, NY, 4, PIECE, QCOLS), BF),
             pltpu.VMEM((4, PIECE, QCOLS), BF),
             pltpu.VMEM((4, BLK, NZ * NY * PIECE), BF),
+            pltpu.VMEM((QCOLS, NZ * NY * PIECE), BF),
+            pltpu.VMEM((BLK, QCOLS), BF),
             pltpu.VMEM((HEADS * BLK, HD), F32),
             pltpu.VMEM((HEADS * BLK, 2 * HD), F32),
             DMA((5,)), DMA((8,)), DMA((8,)), DMA((NZ,)), DMA((NZ,)), DMA((2,)), DMA((2,)),
             DMA((3,)), DMA((3,)),
-            DMA((3,)), DMA((3,)), DMA((2,)), DMA((2,)), DMA((2,)), DMA((2,)),
+            DMA((3,)), DMA((3,)), DMA((2, 2)), DMA((2, 2)), DMA((2,)), DMA((2,)), DMA, DMA,
             *SPREAD_SEMS, *RING_SEMS, *RING_SEMS,
         ],
         compiler_params=pltpu.CompilerParams(
@@ -641,17 +661,8 @@
     )(patch_rows, q_text, kv_text, image_count[None, :], w_out)
 
 
-def swap_core(value):
-    pairs = []
-    for ctx in range(lax.axis_size("ctx")):
-        for tp in range(lax.axis_size("tp")):
-            xh, core = ctx % 2, tp % 2
-            pairs.append((ctx * 4 + tp, (ctx - xh + core) * 4 + tp - core + xh))
-    return lax.ppermute(value, ("ctx", "tp"), pairs)
-
-
 def body(q_text, kv_text, patch_rows, image_count, w_out):
-    return swap_core(layer(q_text, kv_text, patch_rows, image_count, w_out))
+    return layer(q_text, kv_text, patch_rows, image_count, w_out)
 
 
 def solution(mesh):

time: 132 us -> 127 us (0.962)
  starting transfers between devices: 4.63 us -> 0 us
  waiting for transfers between devices: 4.42 us -> 0 us
  Pallas kernels: 122 us -> 126 us
    ppermute x1 -> x0, starting transfers between devices: 4.63 us -> none  [swap_core(): return lax.ppermute(value, ('ctx', 'tp'), pairs)]
    ppermute x1 -> x0, waiting for transfers between devices: 4.42 us -> none  [swap_core(): return lax.ppermute(value, ('ctx', 'tp'), pairs)]
    pallas_call x1, Pallas kernels: 122 us -> 126 us  [layer(): pl.pallas_call(layer_kernel, out_shape=jax.ShapeDtypeStruct((BLK, QCOLS),...]
  transfers between devices with their start and end apart: 1 -> 0, of which waited for: 1 -> 0; matrix products, arithmetic and copies ran while one was open for 0% -> 0% of each run, Pallas kernels for 0% -> 0%
where the time goes in v6:
time: 127 us
  Pallas kernels  126 us (99%)
  local copies, waits for them, and re-layouts  1.65 us (1%)
    pallas_call x1, Pallas kernels, layer(): pl.pallas_call(layer_kernel, out_shape=jax.ShapeDtypeStruct((BLK, QCOLS),...  126 us

profile of v6, /device:TPU:1, one launch (start us, length us, event | category | flops | bytes accessed | tf_op | source)
XLA Modules:
  0.0 127.2 jit_solution(11791335824706296604)
XLA Ops:
  0.0 125.5 %layer.1 = bf16[128,896]{1,0:T(8,128)(2,1)} custom-call(bf16[64,1152]{1,0:T(8,128)(2,1)} %patch_hbm.1, bf16[128,896]{1,0:T(8,128)(2,1)} %q_ref.1, bf16[128,256]{1,0:T(8,128)(2,1)} %kv_ref.1, s32[1,128]{1,0:T(1,128)} %bitcast.1, bf16[7,3584]{1,0:T(8,128)(2,1)} %w_out_hbm.1), custom_call_target="tpu_custom_call" | custom-call | tf_op jit(solution)/shard_map/layer/pallas_call | solution.py:630
  125.5 1.6 %copy.7 = bf16[128,896]{1,0:T(8,128)(2,1)} copy(bf16[128,896]{1,0:T(8,128)(2,1)} %layer.1) | data formatting | bytes 458752

commit v7 on v6

--- a/solution.py
+++ b/solution.py
@@ -472,8 +472,6 @@
 
     for ring in rings:
         ring.set_off()
-    for ring in rings:
-        ring.step(1)
 
     @pl.when(straight)
     def _():
@@ -499,6 +497,8 @@
     kv_swap().start()
     keys_values.waits(buf.at[p.z, p.y, 1 - p.core], c_recv.at[2])
     keys_values.begin()
+    for ring in rings:
+        ring.step(1)
 
     def attend(group, masked):
         block = buf[group].reshape(2 * NY * BLK, 2 * HD)

time: 127 us -> 126 us (level)
  Pallas kernels: 126 us -> 124 us
where the time goes in v7:
time: 126 us
  Pallas kernels  124 us (98%)
  local copies, waits for them, and re-layouts  1.65 us (1%)
    pallas_call x1, Pallas kernels, layer(): pl.pallas_call(layer_kernel, out_shape=jax.ShapeDtypeStruct((BLK, QCOLS),...  124 us

profile of v7, /device:TPU:1, one launch (start us, length us, event | category | flops | bytes accessed | tf_op | source)
XLA Modules:
  0.0 126.0 jit_solution(7647468752154250549)
XLA Ops:
  0.0 124.3 %layer.1 = bf16[128,896]{1,0:T(8,128)(2,1)} custom-call(bf16[64,1152]{1,0:T(8,128)(2,1)} %patch_hbm.1, bf16[128,896]{1,0:T(8,128)(2,1)} %q_ref.1, bf16[128,256]{1,0:T(8,128)(2,1)} %kv_ref.1, s32[1,128]{1,0:T(1,128)} %bitcast.1, bf16[7,3584]{1,0:T(8,128)(2,1)} %w_out_hbm.1), custom_call_target="tpu_custom_call" | custom-call | tf_op jit(solution)/shard_map/layer/pallas_call | solution.py:630
  124.3 1.6 %copy.7 = bf16[128,896]{1,0:T(8,128)(2,1)} copy(bf16[128,896]{1,0:T(8,128)(2,1)} %layer.1) | data formatting | bytes 458752
